TPU v7x, 256 devices: a whole 4x4x8 slice. The times are simulated.
256 devices in a mesh: path: 32 (over y, x, core), shard: 8 (over z).
Axes of the slice: x: 4, y: 4, z: 8, core: 2. Of those that a mesh axis runs over, the one named last changes fastest.
Arguments:
- trained: bfloat16 [32, 4096, 2048], P('path', 'shard'), may hold values from -0.09375 to 0.09375
- outer_params: float32 [8, 8, 512, 2048], P(None, 'shard', 'path'), may hold values from -0.09375 to 0.09375
- momentum: float32 [8, 8, 512, 2048], P(None, 'shard', 'path'), may hold values from -0.12 to 0.12
- path_module: int32 [32, 1], replicated, may hold values from 0 to 7
- module_slot: int32 [8], replicated, may hold values from 0 to 7, each once
- hidden: bfloat16 [32, 2048, 4096], P('path', None, 'shard'), may hold values from -6 to 6
- residual: bfloat16 [32, 2048, 2048], P('path', 'shard'), may hold values from -6 to 6
Outputs:
- new_params: float32 [8, 8, 512, 2048], P(None, 'shard', 'path')
- new_momentum: float32 [8, 8, 512, 2048], P(None, 'shard', 'path')
- new_slabs: bfloat16 [32, 4096, 2048], P('path', 'shard')
- mixed: bfloat16 [32, 2048, 2048], P('path', 'shard')
Inputs may be any that keep to these rules, and one draw needn't show every extreme that they name: `path_module`: every module is used by at least one path. `module_slot`: each slot holds exactly one module.
All inputs are finite; a program needn't handle non-finite values.
Results may differ from a plain program's by a relative error of at most 0.015.
Values may be sent and summed in bfloat16 or wider, within the bound.
No kernel may reach another device: no remote copies, remote signals or barrier semaphores. Data moves between devices by JAX's collectives and lax.ppermute only.
A program may use at most 128 MiB of HBM per device.

v0:
```python
import jax
import jax.numpy as jnp
from jax import lax
from jax.sharding import PartitionSpec as P


def body(trained, outer_params, momentum, path_module, module_slot, hidden, residual):
    paths = lax.axis_size("path")
    mods = outer_params.shape[0]
    piece = outer_params.shape[2]
    width = outer_params.shape[3]
    labels = jnp.arange(mods, dtype=jnp.int32)
    slot_of_path = jnp.sum(
        jnp.where(path_module == labels[None, :], module_slot[None, :], 0), axis=1
    )
    choose = slot_of_path[None, :] == labels[:, None]
    counts = jnp.sum(choose.astype(jnp.float32), axis=1)
    local = trained.reshape(paths, piece, width)
    received = lax.all_to_all(local, "path", split_axis=0, concat_axis=0, tiled=True)
    totals = jnp.einsum(
        "kj,jrd->krd", choose.astype(jnp.bfloat16), received, preferred_element_type=jnp.float32
    )
    average = (totals / counts[:, None, None]).reshape(outer_params.shape)
    pseudo = outer_params - average
    new_momentum = 0.9 * momentum + pseudo
    new_params = outer_params - 0.7 * (pseudo + 0.9 * new_momentum)
    weights = new_params.astype(jnp.bfloat16).reshape(mods, piece, width)
    everything = lax.all_gather(weights, "path", axis=1, tiled=True)
    own_slot = jnp.sum(
        jnp.where(jnp.arange(paths, dtype=jnp.int32) == lax.axis_index("path"), slot_of_path, 0)
    )
    slab = lax.dynamic_index_in_dim(everything, own_slot, 0, keepdims=False)
    rows_in = hidden[0]
    summed = lax.psum_scatter(
        jnp.dot(rows_in, slab, preferred_element_type=jnp.float32).astype(jnp.bfloat16),
        "shard",
        scatter_dimension=0,
        tiled=True,
    ).astype(jnp.float32)
    mixed = (residual[0].astype(jnp.float32) + summed).astype(jnp.bfloat16)
    return (new_params, new_momentum, slab[None], mixed[None])


def solution(mesh):
    placed = (
        P("path", "shard", None),
        P(None, "shard", "path", None),
        P(None, "shard", "path", None),
        P(),
        P(),
        P("path", None, "shard"),
        P("path", "shard", None),
    )
    return jax.shard_map(
        body,
        mesh=mesh,
        in_specs=placed,
        out_specs=(
            P(None, "shard", "path", None),
            P(None, "shard", "path", None),
            P("path", "shard", None),
            P("path", "shard", None),
        ),
        check_vma=False,
    )
```

profile of v0, /device:TPU:6, one launch (start us, length us, event | category | flops | bytes accessed | tf_op | source)
XLA Modules:
  0.0 253.7 jit_solution(6608296072569454080)
XLA Ops:
  7.2 0.0 copy-start
  7.2 0.0 copy-start.4
  7.2 0.0 copy-start.5
  7.2 0.0 copy-start.3
  7.2 7.9 %all-to-all-start = ((bf16[32,16,2048]{2,1,0:T(8,128)(2,1)}), bf16[32,16,2048]{2,1,0:T(8,128)(2,1)}, u32[]{:S(2)}, u32[]{:S(2)}) async-start(bf16[32,16,2048]{2,1,0:T(8,128)(2,1)} %bitcast.32), calls=%async_computation | async-start | bytes 4194304 | tf_op jit(solution)/shard_map/all_to_all | solution.py:19
  15.1 0.0 all-gather.3.cloned.1.call-start
  15.2 0.0 copy-done.4
  15.2 0.0 copy-done.5
  15.2 0.1 select_reduce_fusion
  15.3 0.1 convert_reduce_fusion
  15.4 25.3 %all-to-all-done = bf16[32,16,2048]{2,1,0:T(8,128)(2,1)} async-done(((bf16[32,16,2048]{2,1,0:T(8,128)(2,1)}), bf16[32,16,2048]{2,1,0:T(8,128)(2,1)}, u32[]{:S(2)}, u32[]{:S(2)}) %all-to-all-start) | async-done | bytes 2097184 | tf_op jit(solution)/shard_map/all_to_all | solution.py:19
  40.7 0.0 copy-done.3
  40.7 6.9 %convert_bitcast_fusion.1 = (bf16[8,1,16,2048]{3,0,1,2:T(8,128)(2,1)}, f32[8,1,16,2048]{3,0,2,1:T(8,128)}, f32[8,1,16,2048]{3,0,2,1:T(8,128)}) fusion(f32[8,1,16,2048]{3,2,1,0:T(8,128)S(1)} %copy-done.3, f32[8,1,16,2048]{3,2,1,0:T(8,128)} %param.8, f32[8]{0:T(128)S(1)} %convert_reduce_fusion, bf16[32,16,2048]{2,1,0:T(8,128)(2,1)} %all-to-all-done, ...), kind=kOutput, calls=%fused_computation.15 | convolution fusion | flops 19136768 | bytes 6815904 | tf_op jit(solution)/shard_map/kj,jrd->krd/dot_general | solution.py:20
  47.6 0.0 all-gather.3.cloned.1.call-update
  47.7 0.2 reduce-scatter.2.cloned.1.call-start
  47.9 0.6 fusion.12
  50.5 77.7 %all-gather.3.cloned.1.call-done = bf16[8,1,512,2048]{3,0,1,2:T(8,128)(2,1)} async-done(((bf16[8,1,16,2048]{3,0,1,2:T(8,128)(2,1)}), bf16[8,1,512,2048]{3,0,1,2:T(8,128)(2,1)}) %all-gather.3.cloned.1.call-update) | async-done | bytes 16777232 | tf_op jit(solution)/shard_map/all_gather | solution.py:28
  128.1 7.4 %constant_dynamic-slice_fusion = bf16[1,1,512,2048]{3,0,1,2:T(2,128)(2,1)S(1)} fusion(bf16[8,1,512,2048]{3,0,1,2:T(8,128)(2,1)} %all-gather.3.cloned.1.call-done, s32[]{:T(128)S(6)} %select_n.14), kind=kLoop, calls=%fused_computation.24 | loop fusion | bytes 4194308 | tf_op jit(solution)/shard_map/jit(dynamic_index_in_dim)/dynamic_slice | solution.py:32
  135.5 0.0 copy-start.1
  135.6 1.9 copy-done.1
  137.5 0.0 copy-done
  137.5 9.9 %convert_bitcast_fusion = bf16[2048,2048]{0,1:T(8,128)(2,1)} fusion(bf16[1,2048,512]{2,1,0:T(8,128)(2,1)S(1)} %copy-done, bf16[1,1,512,2048]{3,0,1,2:T(2,128)(2,1)S(1)} %constant_dynamic-slice_fusion), kind=kOutput, calls=%fused_computation | convolution fusion | flops 4299161600 | bytes 12582912 | tf_op jit(solution)/shard_map/dot_general | solution.py:35
  147.4 0.0 reduce-scatter.2.cloned.1.call-update
  147.5 1.5 copy.42
  148.9 0.0 copy-start.2
  149.0 3.0 %copy.43 = f32[8,1,16,2048]{3,2,1,0:T(8,128)} copy(f32[8,1,16,2048]{3,0,2,1:T(8,128)} %get-tuple-element.21) | data formatting | bytes 2097152
  151.9 2.8 %copy.44 = f32[8,1,16,2048]{3,2,1,0:T(8,128)} copy(f32[8,1,16,2048]{3,0,2,1:T(8,128)} %get-tuple-element.22) | data formatting | bytes 2097152
  154.7 0.0 copy-done.2
  154.7 2.6 %copy.67 = bf16[1,1,512,2048]{3,2,1,0:T(8,128)(2,1)} copy(bf16[1,1,512,2048]{3,0,1,2:T(2,128)(2,1)S(1)} %copy-done.2) | data formatting | bytes 4194304
  157.3 84.8 %reduce-scatter.2.cloned.1.call-done = bf16[256,2048]{0,1:T(8,128)(2,1)} async-done(((bf16[2048,2048]{0,1:T(8,128)(2,1)}), bf16[256,2048]{0,1:T(8,128)(2,1)}) %reduce-scatter.2.cloned.1.call-update) | async-done | bytes 1048592 | tf_op jit(solution)/shard_map/reduce_scatter | solution.py:34
  242.1 2.5 fusion.6
  244.5 2.3 copy.45
Async XLA Ops:
  7.2 130.3 %copy-start = (bf16[1,2048,512]{2,1,0:T(8,128)(2,1)S(1)}, bf16[1,2048,512]{2,1,0:T(8,128)(2,1)}, u32[]{:S(2)}) copy-start(bf16[1,2048,512]{2,1,0:T(8,128)(2,1)} %param.12) | copy-start | bytes 6291460
  7.2 8.0 %copy-start.4 = (s32[8]{0:T(128)S(1)}, s32[8]{0:T(128)}, u32[]{:S(2)}) copy-start(s32[8]{0:T(128)} %param.11) | copy-start | bytes 100
  7.2 8.0 %copy-start.5 = (s32[32,1]{0,1:T(1,128)S(1)}, s32[32,1]{0,1:T(1,128)}, u32[]{:S(2)}) copy-start(s32[32,1]{0,1:T(1,128)} %param.10) | copy-start | bytes 388
  7.2 33.5 %copy-start.3 = (f32[8,1,16,2048]{3,2,1,0:T(8,128)S(1)}, f32[8,1,16,2048]{3,2,1,0:T(8,128)}, u32[]{:S(2)}) copy-start(f32[8,1,16,2048]{3,2,1,0:T(8,128)} %param.9) | copy-start | bytes 3145732
  7.2 33.5 %all-to-all-start = ((bf16[32,16,2048]{2,1,0:T(8,128)(2,1)}), bf16[32,16,2048]{2,1,0:T(8,128)(2,1)}, u32[]{:S(2)}, u32[]{:S(2)}) async-start(bf16[32,16,2048]{2,1,0:T(8,128)(2,1)} %bitcast.32), calls=%async_computation | async-start | bytes 4194304 | tf_op jit(solution)/shard_map/all_to_all | solution.py:19
  15.1 113.0 %all-gather.3.cloned.1.call-start = ((), (), s32[]{:S(2)}) async-start(), calls=%async_computation.3 | async-start | bytes 17301504 | tf_op jit(solution)/shard_map/all_gather | solution.py:28
  47.7 194.4 %reduce-scatter.2.cloned.1.call-start = ((), (), s32[]{:S(2)}) async-start(), calls=%async_computation.2 | async-start | bytes 9437184 | tf_op jit(solution)/shard_map/reduce_scatter | solution.py:34
  135.5 1.9 copy-start.1
  148.9 5.8 %copy-start.2 = (bf16[1,1,512,2048]{3,0,1,2:T(2,128)(2,1)S(1)}, bf16[1,1,512,2048]{3,0,1,2:T(2,128)(2,1)}, u32[]{:S(2)}) copy-start(bf16[1,1,512,2048]{3,0,1,2:T(2,128)(2,1)} %copy-done.1) | copy-start | bytes 6291460
Sparse Core Ops, SparseCore 0:
  47.8 80.3 all-gather.2
  147.6 94.4 reduce-scatter.1
where the time goes:
time: 255 us; the launch traced here: 254 us
  waiting for transfers between devices  188 us (74%)
  local copies, waits for them, and re-layouts  21.5 us (8%)
  matrix products  16.8 us (7%)
  between operations  16.1 us (6%)
  starting transfers between devices  8.16 us (3%)
  other arithmetic  3.29 us (1%)
    reduce_scatter x1, waiting for transfers between devices, body(): lax.psum_scatter(jnp.dot(rows_in, slab, preferred_element_type=jnp.float3...  84.8 us
    all_gather x1, waiting for transfers between devices, body(): everything = lax.all_gather(weights, 'path', axis=1, tiled=True)  77.7 us
    all_to_all x1, waiting for transfers between devices, body(): lax.all_to_all(local, 'path', split_axis=0, concat_axis=0, tiled=True)  25.3 us
    unnamed x17, local copies, waits for them, and re-layouts  14.1 us
    dot_general x1, matrix products, body(): jnp.dot(rows_in, slab, preferred_element_type=jnp.float32)  9.94 us
    all_to_all x1, starting transfers between devices, body(): lax.all_to_all(local, 'path', split_axis=0, concat_axis=0, tiled=True)  7.89 us
    dynamic_slice x1, local copies, waits for them, and re-layouts, body(): slab = lax.dynamic_index_in_dim(everything, own_slot, 0, keepdims=False)  7.39 us
    dot_general x1, matrix products, body(): jnp.einsum('kj,jrd->krd', choose.astype(jnp.bfloat16), received, preferre...  6.89 us
  transfers between devices with their start and end apart: 3, of which 3 were waited for; matrix products, arithmetic and copies ran while one was open for 4% of the time, Pallas kernels for 0%

commit v1 on v0

v1 whole, which is shorter than its diff:
```python
import jax
import jax.numpy as jnp
from jax import lax
from jax.experimental import pallas as pl
from jax.experimental.pallas import tpu as pltpu
from jax.sharding import PartitionSpec as P

STREAMS = (1024, 1024)
HEADS = True
WIDE = 256
LIMIT = 12


def after(value, *others):
    return lax.optimization_barrier((value, *others))[0]


def update_kernel(pick, back, count, received, outer, moment, params, moments, sent):
    totals = jnp.dot(pick[...], received[...], preferred_element_type=jnp.float32)
    pseudo = outer[...] - totals / count[...]
    momentum = 0.9 * moment[...] + pseudo
    new = outer[...] - 0.7 * (pseudo + 0.9 * momentum)
    params[...] = new
    moments[...] = momentum
    sent[...] = jnp.dot(
        back[...], new.astype(jnp.bfloat16), preferred_element_type=jnp.float32
    ).astype(jnp.bfloat16)


def update(pick, back, count, received, outer, moment):
    held, width = outer.shape
    rows = received.shape[0]
    wide = WIDE
    fixed = lambda i: (0, 0)
    here = lambda i: (0, i)
    return pl.pallas_call(
        update_kernel,
        grid=(width // wide,),
        in_specs=[
            pl.BlockSpec(pick.shape, fixed),
            pl.BlockSpec(back.shape, fixed),
            pl.BlockSpec(count.shape, fixed),
            pl.BlockSpec((rows, wide), here),
            pl.BlockSpec((held, wide), here),
            pl.BlockSpec((held, wide), here),
        ],
        out_specs=[
            pl.BlockSpec((held, wide), here),
            pl.BlockSpec((held, wide), here),
            pl.BlockSpec((rows, wide), here),
        ],
        out_shape=[
            pltpu.HBM((held, width), jnp.float32),
            pltpu.HBM((held, width), jnp.float32),
            pltpu.HBM((rows, width), jnp.bfloat16),
        ],
        compiler_params=pltpu.CompilerParams(vmem_limit_bytes=LIMIT * 1024 * 1024),
        cost_estimate=pl.CostEstimate(
            flops=4 * held * rows * width,
            bytes_accessed=(rows * 4 + held * 16) * width,
            transcendentals=0,
        ),
        name="update",
    )(pick, back, count, received, outer, moment)


def product_kernel(place, hidden, slab, *rest):
    outs, slabs, total = rest[-8:-2], rest[-2], rest[-1]
    total[...] = jnp.dot(hidden[...], slab[...], preferred_element_type=jnp.float32).astype(
        total.dtype
    )
    slabs[...] = slab[...]
    tokens = outs[0].shape[0]
    shards = hidden.shape[0] // tokens
    far = shards // 2
    for d, out in zip([d for d in range(shards) if d not in (far, far + 1)], outs):
        start = pl.multiple_of(place[d] * tokens, tokens)
        out[...] = total[pl.ds(start, tokens), :]


def products(place, hidden, slab, earlier, at, w, shards):
    rows, width = slab.shape
    tokens = hidden.shape[0] // shards
    wide = WIDE
    first = at // wide
    outs = pl.pallas_call(
        product_kernel,
        grid_spec=pltpu.PrefetchScalarGridSpec(
            num_scalar_prefetch=1,
            grid=(w // wide,),
            in_specs=[
                pl.BlockSpec(hidden.shape, lambda j, p: (0, 0)),
                pl.BlockSpec((rows, wide), lambda j, p: (0, first + j)),
            ]
            + [pl.BlockSpec(memory_space=pl.ANY)] * len(earlier),
            out_specs=[pl.BlockSpec((tokens, wide), lambda j, p: (0, j))] * (shards - 2)
            + [pl.BlockSpec((rows, wide), lambda j, p: (0, first + j))],
            scratch_shapes=[pltpu.VMEM((hidden.shape[0], wide), jnp.bfloat16)],
        ),
        out_shape=[jax.ShapeDtypeStruct((tokens, w), jnp.bfloat16)] * (shards - 2)
        + [pltpu.HBM((rows, width), jnp.bfloat16)],
        input_output_aliases={3: shards - 2} if earlier else {},
        compiler_params=pltpu.CompilerParams(vmem_limit_bytes=LIMIT * 1024 * 1024),
        cost_estimate=pl.CostEstimate(
            flops=2 * hidden.size * w,
            bytes_accessed=2 * (hidden.size + 2 * rows * w + shards * tokens * w),
            transcendentals=0,
        ),
        name="products",
    )(place, hidden, slab, *earlier)
    return list(outs[:-1]), outs[-1]


def body(trained, outer_params, momentum, path_module, module_slot, hidden, residual):
    paths = lax.axis_size("path")
    shards = lax.axis_size("shard")
    mods = outer_params.shape[0]
    piece = outer_params.shape[2]
    width = outer_params.shape[3]
    rows = paths * piece
    held = mods * piece
    labels = jnp.arange(mods, dtype=jnp.int32)
    slot_of_path = jnp.sum(
        jnp.where(path_module == labels[None, :], module_slot[None, :], 0), axis=1
    )
    choose = slot_of_path[None, :] == labels[:, None]
    counts = jnp.sum(choose.astype(jnp.float32), axis=1)
    count_of_row = jnp.repeat(counts, piece)[:, None]
    row_of_held = jnp.arange(held, dtype=jnp.int32)
    row_of_all = jnp.arange(rows, dtype=jnp.int32)
    slot_of_row = jnp.repeat(slot_of_path, piece) * piece + row_of_all % piece
    pick = (row_of_held[:, None] == slot_of_row[None, :]).astype(jnp.bfloat16)
    back = (slot_of_row[:, None] == row_of_held[None, :]).astype(jnp.bfloat16)

    def exchange(block):
        w = block.shape[1]
        return lax.all_to_all(
            block.reshape(paths, piece, w), "path", split_axis=0, concat_axis=0, tiled=True
        ).reshape(rows, w)

    outer = outer_params.reshape(held, width)
    moment = momentum.reshape(held, width)
    rows_in = hidden[0]
    z = lax.axis_index("shard")
    tokens = residual.shape[1]
    up = [(i, (i + 1) % shards) for i in range(shards)]
    down = [(i, (i - 1) % shards) for i in range(shards)]
    far = shards // 2
    ring_width = sum(STREAMS)

    received = exchange(trained[0])
    params, moments, sent = update(pick, back, count_of_row, received, outer, moment)
    slab = exchange(sent)

    def add(part, value):
        return (part.astype(jnp.float32) + value.astype(jnp.float32)).astype(jnp.bfloat16)

    class Ring:
        def __init__(self, lo, w, flip):
            self.lo, self.w = lo, w
            self.one, self.other = (down, up) if flip else (up, down)
            self.sign = -1 if flip else 1
            self.ahead, self.behind = self.head(far), self.head(far + 1)

        def head(self, offset):
            at = (z + self.sign * offset) % shards * tokens
            block = lax.dynamic_slice_in_dim(rows_in, at, tokens, 0)
            part = jnp.dot(
                block, slab[:, self.lo:self.lo + self.w], preferred_element_type=jnp.float32
            )
            return part.astype(jnp.bfloat16)

        def run(self, slab, earlier):
            place = ((z + self.sign * jnp.arange(shards, dtype=jnp.int32)) % shards).astype(jnp.int32)
            parts, whole = products(place, rows_in, slab, earlier, self.lo, self.w, shards)
            parts = parts[:far] + [None, None] + parts[far:]
            for k in range(far - 1, 0, -1):
                self.ahead = add(parts[k], lax.ppermute(self.ahead, "shard", self.one))
            for k in range(far - 2, 0, -1):
                self.behind = add(parts[shards - k], lax.ppermute(self.behind, "shard", self.other))
            ahead = lax.ppermute(self.ahead, "shard", self.one)
            behind = lax.ppermute(self.behind, "shard", self.other)
            own = parts[0].astype(jnp.float32)
            own = own + residual[0, :, self.lo:self.lo + self.w].astype(jnp.float32)
            self.total = (own + ahead.astype(jnp.float32) + behind.astype(jnp.float32)).astype(
                jnp.bfloat16
            )
            return [whole]

    rings, lo = [], 0
    for n, w in enumerate(STREAMS):
        rings.append(Ring(lo, w, n % 2 == 1))
        lo += w
    if HEADS:
        later = after(slab, *[r.ahead for r in rings], *[r.behind for r in rings])
    else:
        later = slab
    whole = []
    for r in rings:
        whole = r.run(later, whole)
    mixed = [r.total for r in rings]
    return (
        params.reshape(outer_params.shape),
        moments.reshape(outer_params.shape),
        whole[0][None],
        jnp.concatenate(mixed, axis=1)[None],
    )


def solution(mesh):
    placed = (
        P("path", "shard", None),
        P(None, "shard", "path", None),
        P(None, "shard", "path", None),
        P(),
        P(),
        P("path", None, "shard"),
        P("path", "shard", None),
    )
    return jax.shard_map(
        body,
        mesh=mesh,
        in_specs=placed,
        out_specs=(
            P(None, "shard", "path", None),
            P(None, "shard", "path", None),
            P("path", "shard", None),
            P("path", "shard", None),
        ),
        check_vma=False,
    )
```

time: 255 us -> 175 us (0.69)
  waiting for transfers between devices: 188 us -> 105 us
  starting transfers between devices: 8.16 us -> 43.1 us
  local copies, waits for them, and re-layouts: 21.5 us -> 1.56 us
  Pallas kernels: 0 us -> 15.3 us
  between operations: 16.1 us -> 0.97 us
  matrix products: 16.8 us -> 3.81 us
    reduce_scatter x1 -> x0, waiting for transfers between devices: 84.8 us -> none  [body(): lax.psum_scatter(jnp.dot(rows_in, slab, preferred_element_type=jnp.float3...]
    all_gather x1 -> x0, waiting for transfers between devices: 77.7 us -> none  [body(): everything = lax.all_gather(weights, 'path', axis=1, tiled=True)]
    ppermute x0 -> x14, waiting for transfers between devices: none -> 54.7 us  [the longest x6 29.3 us: run(): self.ahead = add(parts[k], lax.ppermute(self.ahead, 'shard', self.one))]
    ppermute x0 -> x14, starting transfers between devices: none -> 27 us  [the longest x6 11.3 us: run(): self.ahead = add(parts[k], lax.ppermute(self.ahead, 'shard', self.one))]
    all_to_all x1 -> x2, waiting for transfers between devices: 25.3 us -> 50.4 us  [exchange(): lax.all_to_all(block.reshape(paths, piece, w), 'path', split_axis=0, conc...]
    pallas_call x0 -> x3, Pallas kernels: none -> 15.3 us  [the longest x2 9.91 us: products(): pl.pallas_call(product_kernel, grid_spec=pltpu.PrefetchScalarGridSpec(num...]
    dot_general x2 -> x4, matrix products: 16.8 us -> 3.81 us  [head(): jnp.dot(block, slab[:, self.lo:self.lo + self.w], preferred_element_type=...]
    unnamed x17 -> x12, local copies, waits for them, and re-layouts: 14.1 us -> 1.25 us
  transfers between devices with their start and end apart: 3 -> 16, of which waited for: 3 -> 10; matrix products, arithmetic and copies ran while one was open for 4% -> 2% of each run, Pallas kernels for 0% -> 6%
where the time goes in v1:
time: 175 us; the launch traced here: 174 us
  waiting for transfers between devices  105 us (60%)
  starting transfers between devices  43.1 us (25%)
  Pallas kernels  15.3 us (9%)
  other arithmetic  4.23 us (2%)
  matrix products  3.81 us (2%)
    all_to_all x2, waiting for transfers between devices, exchange(): lax.all_to_all(block.reshape(paths, piece, w), 'path', split_axis=0, conc...  50.4 us
    ppermute x6, waiting for transfers between devices, run(): self.ahead = add(parts[k], lax.ppermute(self.ahead, 'shard', self.one))  29.3 us
    all_to_all x2, starting transfers between devices, exchange(): lax.all_to_all(block.reshape(paths, piece, w), 'path', split_axis=0, conc...  16.1 us
    ppermute x4, waiting for transfers between devices, run(): lax.ppermute(self.behind, 'shard', self.other)  14.1 us
    ppermute x6, starting transfers between devices, run(): self.ahead = add(parts[k], lax.ppermute(self.ahead, 'shard', self.one))  11.3 us
    ppermute x2, waiting for transfers between devices, run(): ahead = lax.ppermute(self.ahead, 'shard', self.one)  11.3 us
    pallas_call x2, Pallas kernels, products(): pl.pallas_call(product_kernel, grid_spec=pltpu.PrefetchScalarGridSpec(num...  9.91 us
    ppermute x4, starting transfers between devices, run(): lax.ppermute(self.behind, 'shard', self.other)  7.99 us
  transfers between devices with their start and end apart: 16, of which 10 were waited for; matrix products, arithmetic and copies ran while one was open for 2% of the time, Pallas kernels for 6%

profile of v1, /device:TPU:6, one launch (start us, length us, event | category | flops | bytes accessed | tf_op | source)
XLA Modules:
  0.0 174.1 jit_solution(9612768845447096277)
XLA Ops:
  0.7 7.7 %all-to-all-start = ((bf16[32,16,2048]{2,1,0:T(8,128)(2,1)}), bf16[32,16,2048]{2,1,0:T(8,128)(2,1)S(1)}, u32[]{:S(2)}, u32[]{:S(2)}) async-start(bf16[32,16,2048]{2,1,0:T(8,128)(2,1)} %bitcast.46), calls=%async_computation | async-start | bytes 4194304 | tf_op jit(solution)/shard_map/all_to_all | solution.py:137
  9.1 24.8 %all-to-all-done = bf16[32,16,2048]{2,1,0:T(8,128)(2,1)S(1)} async-done(((bf16[32,16,2048]{2,1,0:T(8,128)(2,1)}), bf16[32,16,2048]{2,1,0:T(8,128)(2,1)S(1)}, u32[]{:S(2)}, u32[]{:S(2)}) %all-to-all-start) | async-done | bytes 2097184 | tf_op jit(solution)/shard_map/all_to_all | solution.py:137
  34.0 1.2 copy-done.1
  35.2 5.4 %update.1 = (f32[128,2048]{1,0:T(8,128)}, f32[128,2048]{1,0:T(8,128)}, bf16[512,2048]{1,0:T(8,128)(2,1)}) custom-call(bf16[128,512]{1,0:T(8,128)(2,1)S(1)} %fusion.18.pick, bf16[512,128]{1,0:T(8,128)(2,1)S(1)} %fusion.19.back, f32[128,1]{1,0:T(8,128)S(1)} %broadcast_in_dim_reshape.4.count, bf16[512,2048]{1,0:T(8,128)(2,1)S(1)} %bitcast.35, ...), custom_call_target="tpu_custom_call" | custom-call | flops 536870912 | bytes 8388608 | tf_op jit(solution)/shard_map/update/pallas_call | solution.py:36
  40.6 8.3 %all-to-all-start.1 = ((bf16[32,16,2048]{2,1,0:T(8,128)(2,1)}), bf16[32,16,2048]{2,1,0:T(8,128)(2,1)S(1)}, u32[]{:S(2)}, u32[]{:S(2)}) async-start(bf16[32,16,2048]{2,1,0:T(8,128)(2,1)} %bitcast.47), calls=%async_computation.1 | async-start | bytes 4194304 | tf_op jit(solution)/shard_map/all_to_all | solution.py:137
  49.1 25.5 %all-to-all-done.1 = bf16[32,16,2048]{2,1,0:T(8,128)(2,1)S(1)} async-done(((bf16[32,16,2048]{2,1,0:T(8,128)(2,1)}), bf16[32,16,2048]{2,1,0:T(8,128)(2,1)S(1)}, u32[]{:S(2)}, u32[]{:S(2)}) %all-to-all-start.1) | async-done | bytes 2097184 | tf_op jit(solution)/shard_map/all_to_all | solution.py:137
  74.6 1.5 convolution_convert_fusion.1
  76.1 1.4 convolution_convert_fusion
  77.6 0.4 convolution_convert_fusion.3
  78.0 2.0 %collective-permute-start = (bf16[256,1024]{1,0:T(8,128)(2,1)S(1)}, bf16[256,1024]{1,0:T(8,128)(2,1)S(1)}, u32[]{:S(2)}, u32[]{:S(2)}) collective-permute-start(bf16[256,1024]{1,0:T(8,128)(2,1)S(1)} %convolution_convert_fusion.3), channel_id=1, source_target_pairs={{0,1},{1,2},{2,3},{3,4},{4,5},{5,6},{6,7},{7,0},{8,9},{9,10},{10,1... | collective-permute-start | bytes 1572872 | tf_op jit(solution)/shard_map/ppermute | solution.py:178
  80.0 0.4 convolution_convert_fusion.2
  80.5 4.0 %collective-permute-start.7 = (bf16[256,1024]{1,0:T(8,128)(2,1)S(1)}, bf16[256,1024]{1,0:T(8,128)(2,1)S(1)}, u32[]{:S(2)}, u32[]{:S(2)}) collective-permute-start(bf16[256,1024]{1,0:T(8,128)(2,1)S(1)} %convolution_convert_fusion.2), channel_id=1, source_target_pairs={{0,7},{1,0},{2,1},{3,2},{4,3},{5,4},{6,5},{7,6},{8,15},{9,8},{10,9... | collective-permute-start | bytes 1572872 | tf_op jit(solution)/shard_map/ppermute | solution.py:178
  84.5 3.2 %collective-permute-start.4 = (bf16[256,1024]{1,0:T(8,128)(2,1)S(1)}, bf16[256,1024]{1,0:T(8,128)(2,1)S(1)}, u32[]{:S(2)}, u32[]{:S(2)}) collective-permute-start(bf16[256,1024]{1,0:T(8,128)(2,1)S(1)} %convolution_convert_fusion.1), channel_id=1, source_target_pairs={{0,7},{1,0},{2,1},{3,2},{4,3},{5,4},{6,5},{7,6},{8,15},{9,8},{10,9... | collective-permute-start | bytes 1572872 | tf_op jit(solution)/shard_map/ppermute | solution.py:180
  87.7 4.9 %products.2 = (bf16[256,1024]{1,0:T(8,128)(2,1)S(1)}, bf16[256,1024]{1,0:T(8,128)(2,1)S(1)}, bf16[256,1024]{1,0:T(8,128)(2,1)S(1)}, bf16[256,1024]{1,0:T(8,128)(...) custom-call(s32[8]{0:T(128)S(1)} %get-tuple-element.54.place, ...), custom_call_target="tpu_custom_call" | custom-call | flops 2147483648 | bytes 8388608 | tf_op jit(solution)/shard_map/products/pallas_call | solution.py:86
  92.7 5.0 %products.3 = (bf16[256,1024]{1,0:T(8,128)(2,1)S(1)}, bf16[256,1024]{1,0:T(8,128)(2,1)S(1)}, bf16[256,1024]{1,0:T(8,128)(2,1)S(1)}, bf16[256,1024]{1,0:T(8,128)(...) custom-call(s32[8]{0:T(128)S(1)} %get-tuple-element.55.place, ...), custom_call_target="tpu_custom_call", output_to_operand_aliasing={{6}: (3, {})} | custom-call | flops 2147483648 | bytes 8388608 | tf_op jit(solution)/shard_map/products/pallas_call | solution.py:86
  97.9 9.1 %collective-permute-done.4 = bf16[256,1024]{1,0:T(8,128)(2,1)S(1)} collective-permute-done((bf16[256,1024]{1,0:T(8,128)(2,1)S(1)}, bf16[256,1024]{1,0:T(8,128)(2,1)S(1)}, u32[]{:S(2)}, u32[]{:S(2)}) %collective-permute-start.4) | collective-permute-done | bytes 524320 | tf_op jit(solution)/shard_map/ppermute | solution.py:180
  107.2 3.8 %collective-permute-start.5 = (bf16[256,1024]{1,0:T(8,128)(2,1)S(1)}, bf16[256,1024]{1,0:T(8,128)(2,1)S(1)}, u32[]{:S(2)}, u32[]{:S(2)}) collective-permute-start(bf16[256,1024]{1,0:T(8,128)(2,1)S(1)} %add_convert_fusion.6), channel_id=1, source_target_pairs={{0,7},{1,0},{2,1},{3,2},{4,3},{5,4},{6,5},{7,6},{8,15},{9,8},{10,9... | collective-permute-start | bytes 1572872 | tf_op jit(solution)/shard_map/ppermute | solution.py:180
  111.2 1.2 collective-permute-start.8
  112.6 1.0 collective-permute-start.12
  113.6 4.3 %collective-permute-done.1 = bf16[256,1024]{1,0:T(8,128)(2,1)S(1)} collective-permute-done((bf16[256,1024]{1,0:T(8,128)(2,1)S(1)}, bf16[256,1024]{1,0:T(8,128)(2,1)S(1)}, u32[]{:S(2)}, u32[]{:S(2)}) %collective-permute-start.1) | collective-permute-done | bytes 524320 | tf_op jit(solution)/shard_map/ppermute | solution.py:178
  118.1 0.3 collective-permute-start.2
  118.4 5.0 %collective-permute-done.5 = bf16[256,1024]{1,0:T(8,128)(2,1)S(1)} collective-permute-done((bf16[256,1024]{1,0:T(8,128)(2,1)S(1)}, bf16[256,1024]{1,0:T(8,128)(2,1)S(1)}, u32[]{:S(2)}, u32[]{:S(2)}) %collective-permute-start.5) | collective-permute-done | bytes 524320 | tf_op jit(solution)/shard_map/ppermute | solution.py:180
  123.5 3.8 %collective-permute-start.6 = (bf16[256,1024]{1,0:T(8,128)(2,1)S(1)}, bf16[256,1024]{1,0:T(8,128)(2,1)S(1)}, u32[]{:S(2)}, u32[]{:S(2)}) collective-permute-start(bf16[256,1024]{1,0:T(8,128)(2,1)S(1)} %add_convert_fusion.5), channel_id=1, source_target_pairs={{0,7},{1,0},{2,1},{3,2},{4,3},{5,4},{6,5},{7,6},{8,15},{9,8},{10,9... | collective-permute-start | bytes 1572872 | tf_op jit(solution)/shard_map/ppermute | solution.py:182
  127.3 7.3 %collective-permute-done.8 = bf16[256,1024]{1,0:T(8,128)(2,1)S(1)} collective-permute-done((bf16[256,1024]{1,0:T(8,128)(2,1)S(1)}, bf16[256,1024]{1,0:T(8,128)(2,1)S(1)}, u32[]{:S(2)}, u32[]{:S(2)}) %collective-permute-start.8) | collective-permute-done | bytes 524320 | tf_op jit(solution)/shard_map/ppermute | solution.py:178
  134.8 3.8 %collective-permute-start.9 = (bf16[256,1024]{1,0:T(8,128)(2,1)S(1)}, bf16[256,1024]{1,0:T(8,128)(2,1)S(1)}, u32[]{:S(2)}, u32[]{:S(2)}) collective-permute-start(bf16[256,1024]{1,0:T(8,128)(2,1)S(1)} %add_convert_fusion.3), channel_id=1, source_target_pairs={{0,7},{1,0},{2,1},{3,2},{4,3},{5,4},{6,5},{7,6},{8,15},{9,8},{10,9... | collective-permute-start | bytes 1572872 | tf_op jit(solution)/shard_map/ppermute | solution.py:178
  138.8 1.5 collective-permute-done.2
  140.6 16.2 %collective-permute-done.9 = bf16[256,1024]{1,0:T(8,128)(2,1)S(1)} collective-permute-done((bf16[256,1024]{1,0:T(8,128)(2,1)S(1)}, bf16[256,1024]{1,0:T(8,128)(2,1)S(1)}, u32[]{:S(2)}, u32[]{:S(2)}) %collective-permute-start.9) | collective-permute-done | bytes 524320 | tf_op jit(solution)/shard_map/ppermute | solution.py:178
  157.1 3.8 %collective-permute-start.10 = (bf16[256,1024]{1,0:T(8,128)(2,1)S(1)}, bf16[256,1024]{1,0:T(8,128)(2,1)S(1)}, u32[]{:S(2)}, u32[]{:S(2)}) collective-permute-start(bf16[256,1024]{1,0:T(8,128)(2,1)S(1)} %add_convert_fusion.2), channel_id=1, source_target_pairs={{0,7},{1,0},{2,1},{3,2},{4,3},{5,4},{6,5},{7,6},{8,15},{9,8},{10,9... | collective-permute-start | bytes 1572872 | tf_op jit(solution)/shard_map/ppermute | solution.py:181
  160.9 3.8 %collective-permute-done.3 = bf16[256,1024]{1,0:T(8,128)(2,1)S(1)} collective-permute-done((bf16[256,1024]{1,0:T(8,128)(2,1)S(1)}, bf16[256,1024]{1,0:T(8,128)(2,1)S(1)}, u32[]{:S(2)}, u32[]{:S(2)}) %collective-permute-start.3) | collective-permute-done | bytes 524320 | tf_op jit(solution)/shard_map/ppermute | solution.py:181
  164.6 7.5 %collective-permute-done.10 = bf16[256,1024]{1,0:T(8,128)(2,1)S(1)} collective-permute-done((bf16[256,1024]{1,0:T(8,128)(2,1)S(1)}, bf16[256,1024]{1,0:T(8,128)(2,1)S(1)}, u32[]{:S(2)}, u32[]{:S(2)}) %collective-permute-start.10) | collective-permute-done | bytes 524320 | tf_op jit(solution)/shard_map/ppermute | solution.py:181
  172.2 0.9 fusion.5
  173.1 1.0 maximum_bitcast_fusion
  (42 shorter events, 2.9 us)
Async XLA Ops:
  0.6 7.7 %copy-start.4 = (s32[8]{0:T(128)S(1)}, s32[8]{0:T(128)}, u32[]{:S(2)}) copy-start(s32[8]{0:T(128)} %param.11) | copy-start | bytes 100
  0.6 7.7 %copy-start.5 = (s32[32,1]{0,1:T(1,128)S(1)}, s32[32,1]{0,1:T(1,128)}, u32[]{:S(2)}) copy-start(s32[32,1]{0,1:T(1,128)} %param.10) | copy-start | bytes 388
  0.7 33.3 %copy-start = (f32[8,1,16,2048]{3,2,1,0:T(8,128)S(1)}, f32[8,1,16,2048]{3,2,1,0:T(8,128)}, u32[]{:S(2)}) copy-start(f32[8,1,16,2048]{3,2,1,0:T(8,128)} %param.8) | copy-start | bytes 3145732
  0.7 33.3 %all-to-all-start = ((bf16[32,16,2048]{2,1,0:T(8,128)(2,1)}), bf16[32,16,2048]{2,1,0:T(8,128)(2,1)S(1)}, u32[]{:S(2)}, u32[]{:S(2)}) async-start(bf16[32,16,2048]{2,1,0:T(8,128)(2,1)} %bitcast.46), calls=%async_computation | async-start | bytes 4194304 | tf_op jit(solution)/shard_map/all_to_all | solution.py:137
  34.0 1.2 copy-start.1
  40.6 34.0 %all-to-all-start.1 = ((bf16[32,16,2048]{2,1,0:T(8,128)(2,1)}), bf16[32,16,2048]{2,1,0:T(8,128)(2,1)S(1)}, u32[]{:S(2)}, u32[]{:S(2)}) async-start(bf16[32,16,2048]{2,1,0:T(8,128)(2,1)} %bitcast.47), calls=%async_computation.1 | async-start | bytes 4194304 | tf_op jit(solution)/shard_map/all_to_all | solution.py:137
  74.6 3.0 %copy-start.2 = (bf16[1,2048,512]{2,1,0:T(8,128)(2,1)S(1)}, bf16[1,2048,512]{2,1,0:T(8,128)(2,1)}, u32[]{:S(2)}) copy-start(bf16[1,2048,512]{2,1,0:T(8,128)(2,1)} %param.12) | copy-start | bytes 6291460
  78.0 19.6 %collective-permute-start = (bf16[256,1024]{1,0:T(8,128)(2,1)S(1)}, bf16[256,1024]{1,0:T(8,128)(2,1)S(1)}, u32[]{:S(2)}, u32[]{:S(2)}) collective-permute-start(bf16[256,1024]{1,0:T(8,128)(2,1)S(1)} %convolution_convert_fusion.3), channel_id=1, source_target_pairs={{0,1},{1,2},{2,3},{3,4},{4,5},{5,6},{6,7},{7,0},{8,9},{9,10},{10,1... | collective-permute-start | bytes 1572872 | tf_op jit(solution)/shard_map/ppermute | solution.py:178
  80.5 30.6 %collective-permute-start.7 = (bf16[256,1024]{1,0:T(8,128)(2,1)S(1)}, bf16[256,1024]{1,0:T(8,128)(2,1)S(1)}, u32[]{:S(2)}, u32[]{:S(2)}) collective-permute-start(bf16[256,1024]{1,0:T(8,128)(2,1)S(1)} %convolution_convert_fusion.2), channel_id=1, source_target_pairs={{0,7},{1,0},{2,1},{3,2},{4,3},{5,4},{6,5},{7,6},{8,15},{9,8},{10,9... | collective-permute-start | bytes 1572872 | tf_op jit(solution)/shard_map/ppermute | solution.py:178
  84.5 27.9 %collective-permute-start.11 = (bf16[256,1024]{1,0:T(8,128)(2,1)S(1)}, bf16[256,1024]{1,0:T(8,128)(2,1)S(1)}, u32[]{:S(2)}, u32[]{:S(2)}) collective-permute-start(bf16[256,1024]{1,0:T(8,128)(2,1)S(1)} %convolution_convert_fusion), channel_id=1, source_target_pairs={{0,1},{1,2},{2,3},{3,4},{4,5},{5,6},{6,7},{7,0},{8,9},{9,10},{10,1... | collective-permute-start | bytes 1572872 | tf_op jit(solution)/shard_map/ppermute | solution.py:180
  84.5 22.6 %collective-permute-start.4 = (bf16[256,1024]{1,0:T(8,128)(2,1)S(1)}, bf16[256,1024]{1,0:T(8,128)(2,1)S(1)}, u32[]{:S(2)}, u32[]{:S(2)}) collective-permute-start(bf16[256,1024]{1,0:T(8,128)(2,1)S(1)} %convolution_convert_fusion.1), channel_id=1, source_target_pairs={{0,7},{1,0},{2,1},{3,2},{4,3},{5,4},{6,5},{7,6},{8,15},{9,8},{10,9... | collective-permute-start | bytes 1572872 | tf_op jit(solution)/shard_map/ppermute | solution.py:180
  97.8 20.0 %collective-permute-start.1 = (bf16[256,1024]{1,0:T(8,128)(2,1)S(1)}, bf16[256,1024]{1,0:T(8,128)(2,1)S(1)}, u32[]{:S(2)}, u32[]{:S(2)}) collective-permute-start(bf16[256,1024]{1,0:T(8,128)(2,1)S(1)} %add_convert_fusion.9), channel_id=1, source_target_pairs={{0,1},{1,2},{2,3},{3,4},{4,5},{5,6},{6,7},{7,0},{8,9},{9,10},{10,1... | collective-permute-start | bytes 1572872 | tf_op jit(solution)/shard_map/ppermute | solution.py:178
  107.2 16.1 %collective-permute-start.5 = (bf16[256,1024]{1,0:T(8,128)(2,1)S(1)}, bf16[256,1024]{1,0:T(8,128)(2,1)S(1)}, u32[]{:S(2)}, u32[]{:S(2)}) collective-permute-start(bf16[256,1024]{1,0:T(8,128)(2,1)S(1)} %add_convert_fusion.6), channel_id=1, source_target_pairs={{0,7},{1,0},{2,1},{3,2},{4,3},{5,4},{6,5},{7,6},{8,15},{9,8},{10,9... | collective-permute-start | bytes 1572872 | tf_op jit(solution)/shard_map/ppermute | solution.py:180
  111.2 23.3 %collective-permute-start.8 = (bf16[256,1024]{1,0:T(8,128)(2,1)S(1)}, bf16[256,1024]{1,0:T(8,128)(2,1)S(1)}, u32[]{:S(2)}, u32[]{:S(2)}) collective-permute-start(bf16[256,1024]{1,0:T(8,128)(2,1)S(1)} %add_convert_fusion.4), channel_id=1, source_target_pairs={{0,7},{1,0},{2,1},{3,2},{4,3},{5,4},{6,5},{7,6},{8,15},{9,8},{10,9... | collective-permute-start | bytes 1572872 | tf_op jit(solution)/shard_map/ppermute | solution.py:178
  112.6 25.9 %collective-permute-start.12 = (bf16[256,1024]{1,0:T(8,128)(2,1)S(1)}, bf16[256,1024]{1,0:T(8,128)(2,1)S(1)}, u32[]{:S(2)}, u32[]{:S(2)}) collective-permute-start(bf16[256,1024]{1,0:T(8,128)(2,1)S(1)} %add_convert_fusion.1), channel_id=1, source_target_pairs={{0,1},{1,2},{2,3},{3,4},{4,5},{5,6},{6,7},{7,0},{8,9},{9,10},{10,1... | collective-permute-start | bytes 1572872 | tf_op jit(solution)/shard_map/ppermute | solution.py:180
  118.1 22.3 %collective-permute-start.2 = (bf16[256,1024]{1,0:T(8,128)(2,1)S(1)}, bf16[256,1024]{1,0:T(8,128)(2,1)S(1)}, u32[]{:S(2)}, u32[]{:S(2)}) collective-permute-start(bf16[256,1024]{1,0:T(8,128)(2,1)S(1)} %add_convert_fusion.8), channel_id=1, source_target_pairs={{0,1},{1,2},{2,3},{3,4},{4,5},{5,6},{6,7},{7,0},{8,9},{9,10},{10,1... | collective-permute-start | bytes 1572872 | tf_op jit(solution)/shard_map/ppermute | solution.py:178
  123.5 37.3 %collective-permute-start.6 = (bf16[256,1024]{1,0:T(8,128)(2,1)S(1)}, bf16[256,1024]{1,0:T(8,128)(2,1)S(1)}, u32[]{:S(2)}, u32[]{:S(2)}) collective-permute-start(bf16[256,1024]{1,0:T(8,128)(2,1)S(1)} %add_convert_fusion.5), channel_id=1, source_target_pairs={{0,7},{1,0},{2,1},{3,2},{4,3},{5,4},{6,5},{7,6},{8,15},{9,8},{10,9... | collective-permute-start | bytes 1572872 | tf_op jit(solution)/shard_map/ppermute | solution.py:182
  134.8 22.1 %collective-permute-start.9 = (bf16[256,1024]{1,0:T(8,128)(2,1)S(1)}, bf16[256,1024]{1,0:T(8,128)(2,1)S(1)}, u32[]{:S(2)}, u32[]{:S(2)}) collective-permute-start(bf16[256,1024]{1,0:T(8,128)(2,1)S(1)} %add_convert_fusion.3), channel_id=1, source_target_pairs={{0,7},{1,0},{2,1},{3,2},{4,3},{5,4},{6,5},{7,6},{8,15},{9,8},{10,9... | collective-permute-start | bytes 1572872 | tf_op jit(solution)/shard_map/ppermute | solution.py:178
  138.5 33.6 %copy-start.3 = (bf16[1,256,2048]{2,1,0:T(8,128)(2,1)S(1)}, bf16[1,256,2048]{2,1,0:T(8,128)(2,1)}, u32[]{:S(2)}) copy-start(bf16[1,256,2048]{2,1,0:T(8,128)(2,1)} %param.13) | copy-start | bytes 3145732
  138.7 22.1 %collective-permute-start.13 = (bf16[256,1024]{1,0:T(8,128)(2,1)S(1)}, bf16[256,1024]{1,0:T(8,128)(2,1)S(1)}, u32[]{:S(2)}, u32[]{:S(2)}) collective-permute-start(bf16[256,1024]{1,0:T(8,128)(2,1)S(1)} %add_convert_fusion), channel_id=1, source_target_pairs={{0,1},{1,2},{2,3},{3,4},{4,5},{5,6},{6,7},{7,0},{8,9},{9,10},{10,1... | collective-permute-start | bytes 1572872 | tf_op jit(solution)/shard_map/ppermute | solution.py:182
  140.6 24.1 %collective-permute-start.3 = (bf16[256,1024]{1,0:T(8,128)(2,1)S(1)}, bf16[256,1024]{1,0:T(8,128)(2,1)S(1)}, u32[]{:S(2)}, u32[]{:S(2)}) collective-permute-start(bf16[256,1024]{1,0:T(8,128)(2,1)S(1)} %add_convert_fusion.7), channel_id=1, source_target_pairs={{0,1},{1,2},{2,3},{3,4},{4,5},{5,6},{6,7},{7,0},{8,9},{9,10},{10,1... | collective-permute-start | bytes 1572872 | tf_op jit(solution)/shard_map/ppermute | solution.py:181
  157.1 15.1 %collective-permute-start.10 = (bf16[256,1024]{1,0:T(8,128)(2,1)S(1)}, bf16[256,1024]{1,0:T(8,128)(2,1)S(1)}, u32[]{:S(2)}, u32[]{:S(2)}) collective-permute-start(bf16[256,1024]{1,0:T(8,128)(2,1)S(1)} %add_convert_fusion.2), channel_id=1, source_target_pairs={{0,7},{1,0},{2,1},{3,2},{4,3},{5,4},{6,5},{7,6},{8,15},{9,8},{10,9... | collective-permute-start | bytes 1572872 | tf_op jit(solution)/shard_map/ppermute | solution.py:181

commit v2 on v1

--- a/solution.py
+++ b/solution.py
@@ -5,10 +5,10 @@
 from jax.experimental.pallas import tpu as pltpu
 from jax.sharding import PartitionSpec as P
 
-STREAMS = (1024, 1024)
-HEADS = True
+STREAMS = (768, 768, 512)
 WIDE = 256
 LIMIT = 12
+UPW = 512
 
 
 def after(value, *others):
@@ -30,7 +30,7 @@
 def update(pick, back, count, received, outer, moment):
     held, width = outer.shape
     rows = received.shape[0]
-    wide = WIDE
+    wide = UPW
     fixed = lambda i: (0, 0)
     here = lambda i: (0, i)
     return pl.pallas_call(
@@ -174,12 +174,15 @@
             place = ((z + self.sign * jnp.arange(shards, dtype=jnp.int32)) % shards).astype(jnp.int32)
             parts, whole = products(place, rows_in, slab, earlier, self.lo, self.w, shards)
             parts = parts[:far] + [None, None] + parts[far:]
-            for k in range(far - 1, 0, -1):
-                self.ahead = add(parts[k], lax.ppermute(self.ahead, "shard", self.one))
-            for k in range(far - 2, 0, -1):
-                self.behind = add(parts[shards - k], lax.ppermute(self.behind, "shard", self.other))
-            ahead = lax.ppermute(self.ahead, "shard", self.one)
-            behind = lax.ppermute(self.behind, "shard", self.other)
+            ahead, behind = self.ahead, self.behind
+            for k in range(far - 1, -1, -1):
+                ahead = lax.ppermute(ahead, "shard", self.one)
+                if k:
+                    behind = lax.ppermute(behind, "shard", self.other)
+                if k:
+                    ahead = add(parts[k], ahead)
+                if k > 1:
+                    behind = add(parts[shards + 1 - k], behind)
             own = parts[0].astype(jnp.float32)
             own = own + residual[0, :, self.lo:self.lo + self.w].astype(jnp.float32)
             self.total = (own + ahead.astype(jnp.float32) + behind.astype(jnp.float32)).astype(
@@ -191,10 +194,7 @@
     for n, w in enumerate(STREAMS):
         rings.append(Ring(lo, w, n % 2 == 1))
         lo += w
-    if HEADS:
-        later = after(slab, *[r.ahead for r in rings], *[r.behind for r in rings])
-    else:
-        later = slab
+    later = after(slab, *[r.ahead for r in rings], *[r.behind for r in rings])
     whole = []
     for r in rings:
         whole = r.run(later, whole)

time: 175 us -> 173 us (0.989)
  waiting for transfers between devices: 105 us -> 110 us
  starting transfers between devices: 43.1 us -> 38.3 us
    ppermute x14 -> x21, starting transfers between devices: 27 us -> 22.2 us  [the longest x12 13 us: run(): ahead = lax.ppermute(ahead, 'shard', self.one)]
    ppermute x14 -> x21, waiting for transfers between devices: 54.7 us -> 59.3 us  [the longest x12 52.6 us: run(): ahead = lax.ppermute(ahead, 'shard', self.one)]
    pallas_call x1, Pallas kernels: 5.44 us -> 3.48 us  [update(): pl.pallas_call(update_kernel, grid=(width // wide,), in_specs=[pl.BlockSp...]
    pallas_call x2 -> x3, Pallas kernels: 9.91 us -> 10.8 us  [products(): pl.pallas_call(product_kernel, grid_spec=pltpu.PrefetchScalarGridSpec(num...]
    dot_general x4 -> x6, matrix products: 3.81 us -> 4.18 us  [head(): jnp.dot(block, slab[:, self.lo:self.lo + self.w], preferred_element_type=...]
  transfers between devices with their start and end apart: 16 -> 23, of which waited for: 10 -> 11; matrix products, arithmetic and copies ran while one was open for 2% -> 2% of each run, Pallas kernels for 6% -> 6%
where the time goes in v2:
time: 173 us; the launch traced here: 172 us
  waiting for transfers between devices  110 us (64%)
  starting transfers between devices  38.3 us (22%)
  Pallas kernels  14.3 us (8%)
  matrix products  4.18 us (2%)
  other arithmetic  3.34 us (2%)
    ppermute x12, waiting for transfers between devices, run(): ahead = lax.ppermute(ahead, 'shard', self.one)  52.6 us
    all_to_all x2, waiting for transfers between devices, exchange(): lax.all_to_all(block.reshape(paths, piece, w), 'path', split_axis=0, conc...  50.4 us
    all_to_all x2, starting transfers between devices, exchange(): lax.all_to_all(block.reshape(paths, piece, w), 'path', split_axis=0, conc...  16.1 us
    ppermute x12, starting transfers between devices, run(): ahead = lax.ppermute(ahead, 'shard', self.one)  13 us
    pallas_call x3, Pallas kernels, products(): pl.pallas_call(product_kernel, grid_spec=pltpu.PrefetchScalarGridSpec(num...  10.8 us
    ppermute x9, starting transfers between devices, run(): behind = lax.ppermute(behind, 'shard', self.other)  9.21 us
    ppermute x9, waiting for transfers between devices, run(): behind = lax.ppermute(behind, 'shard', self.other)  6.67 us
    dot_general x6, matrix products, head(): jnp.dot(block, slab[:, self.lo:self.lo + self.w], preferred_element_type=...  4.18 us
  transfers between devices with their start and end apart: 23, of which 11 were waited for; matrix products, arithmetic and copies ran while one was open for 2% of the time, Pallas kernels for 6%

profile of v2, /device:TPU:6, one launch (start us, length us, event | category | flops | bytes accessed | tf_op | source)
XLA Modules:
  0.0 172.3 jit_solution(1042563154140669681)
XLA Ops:
  0.7 7.7 %all-to-all-start = ((bf16[32,16,2048]{2,1,0:T(8,128)(2,1)}), bf16[32,16,2048]{2,1,0:T(8,128)(2,1)S(1)}, u32[]{:S(2)}, u32[]{:S(2)}) async-start(bf16[32,16,2048]{2,1,0:T(8,128)(2,1)} %bitcast.58), calls=%async_computation | async-start | bytes 4194304 | tf_op jit(solution)/shard_map/all_to_all | solution.py:137
  9.1 24.8 %all-to-all-done = bf16[32,16,2048]{2,1,0:T(8,128)(2,1)S(1)} async-done(((bf16[32,16,2048]{2,1,0:T(8,128)(2,1)}), bf16[32,16,2048]{2,1,0:T(8,128)(2,1)S(1)}, u32[]{:S(2)}, u32[]{:S(2)}) %all-to-all-start) | async-done | bytes 2097184 | tf_op jit(solution)/shard_map/all_to_all | solution.py:137
  34.0 1.2 copy-done.2
  35.2 3.5 %update.1 = (f32[128,2048]{1,0:T(8,128)}, f32[128,2048]{1,0:T(8,128)}, bf16[512,2048]{1,0:T(8,128)(2,1)}) custom-call(bf16[128,512]{1,0:T(8,128)(2,1)S(1)} %fusion.23.pick, bf16[512,128]{1,0:T(8,128)(2,1)S(1)} %fusion.24.back, f32[128,1]{1,0:T(8,128)S(1)} %broadcast_in_dim_reshape.4.count, bf16[512,2048]{1,0:T(8,128)(2,1)S(1)} %bitcast.54, ...), custom_call_target="tpu_custom_call" | custom-call | flops 536870912 | bytes 8388608 | tf_op jit(solution)/shard_map/update/pallas_call | solution.py:36
  38.7 8.4 %all-to-all-start.1 = ((bf16[32,16,2048]{2,1,0:T(8,128)(2,1)}), bf16[32,16,2048]{2,1,0:T(8,128)(2,1)S(1)}, u32[]{:S(2)}, u32[]{:S(2)}) async-start(bf16[32,16,2048]{2,1,0:T(8,128)(2,1)} %bitcast.59), calls=%async_computation.1 | async-start | bytes 4194304 | tf_op jit(solution)/shard_map/all_to_all | solution.py:137
  47.1 25.5 %all-to-all-done.1 = bf16[32,16,2048]{2,1,0:T(8,128)(2,1)S(1)} async-done(((bf16[32,16,2048]{2,1,0:T(8,128)(2,1)}), bf16[32,16,2048]{2,1,0:T(8,128)(2,1)S(1)}, u32[]{:S(2)}, u32[]{:S(2)}) %all-to-all-start.1) | async-done | bytes 2097184 | tf_op jit(solution)/shard_map/all_to_all | solution.py:137
  72.7 1.4 convolution_convert_fusion.5
  74.1 1.3 convolution_convert_fusion.3
  76.1 2.0 %collective-permute-start.14 = (bf16[256,512]{1,0:T(8,128)(2,1)S(1)}, bf16[256,512]{1,0:T(8,128)(2,1)S(1)}, u32[]{:S(2)}, u32[]{:S(2)}) collective-permute-start(bf16[256,512]{1,0:T(8,128)(2,1)S(1)} %convolution_convert_fusion.5), channel_id=1, source_target_pairs={{0,1},{1,2},{2,3},{3,4},{4,5},{5,6},{6,7},{7,0},{8,9},{9,10},{10,1... | collective-permute-start | bytes 786440 | tf_op jit(solution)/shard_map/ppermute | solution.py:179
  78.1 4.0 %collective-permute-start.18 = (bf16[256,512]{1,0:T(8,128)(2,1)S(1)}, bf16[256,512]{1,0:T(8,128)(2,1)S(1)}, u32[]{:S(2)}, u32[]{:S(2)}) collective-permute-start(bf16[256,512]{1,0:T(8,128)(2,1)S(1)} %convolution_convert_fusion.4), channel_id=1, source_target_pairs={{0,7},{1,0},{2,1},{3,2},{4,3},{5,4},{6,5},{7,6},{8,15},{9,8},{10,9... | collective-permute-start | bytes 786440 | tf_op jit(solution)/shard_map/ppermute | solution.py:181
  82.9 2.0 %collective-permute-start.7 = (bf16[256,768]{1,0:T(8,128)(2,1)S(1)}, bf16[256,768]{1,0:T(8,128)(2,1)S(1)}, u32[]{:S(2)}, u32[]{:S(2)}) collective-permute-start(bf16[256,768]{1,0:T(8,128)(2,1)S(1)} %convolution_convert_fusion.2), channel_id=1, source_target_pairs={{0,7},{1,0},{2,1},{3,2},{4,3},{5,4},{6,5},{7,6},{8,15},{9,8},{10,9... | collective-permute-start | bytes 1179656 | tf_op jit(solution)/shard_map/ppermute | solution.py:179
  85.0 3.1 %collective-permute-start.4 = (bf16[256,768]{1,0:T(8,128)(2,1)S(1)}, bf16[256,768]{1,0:T(8,128)(2,1)S(1)}, u32[]{:S(2)}, u32[]{:S(2)}) collective-permute-start(bf16[256,768]{1,0:T(8,128)(2,1)S(1)} %convolution_convert_fusion.1), channel_id=1, source_target_pairs={{0,7},{1,0},{2,1},{3,2},{4,3},{5,4},{6,5},{7,6},{8,15},{9,8},{10,9... | collective-permute-start | bytes 1179656 | tf_op jit(solution)/shard_map/ppermute | solution.py:181
  88.2 3.9 %products.3 = (bf16[256,768]{1,0:T(8,128)(2,1)S(1)}, bf16[256,768]{1,0:T(8,128)(2,1)S(1)}, bf16[256,768]{1,0:T(8,128)(2,1)S(1)}, bf16[256,768]{1,0:T(8,128)(2,1)...) custom-call(s32[8]{0:T(128)S(1)} %get-tuple-element.69.place, ...), custom_call_target="tpu_custom_call" | custom-call | flops 1610612736 | bytes 6815744 | tf_op jit(solution)/shard_map/products/pallas_call | solution.py:86
  92.0 3.9 %products.4 = (bf16[256,768]{1,0:T(8,128)(2,1)S(1)}, bf16[256,768]{1,0:T(8,128)(2,1)S(1)}, bf16[256,768]{1,0:T(8,128)(2,1)S(1)}, bf16[256,768]{1,0:T(8,128)(2,1)...) custom-call(s32[8]{0:T(128)S(1)} %get-tuple-element.68.place, ...), custom_call_target="tpu_custom_call", output_to_operand_aliasing={{6}: (3, {})} | custom-call | flops 1610612736 | bytes 6815744 | tf_op jit(solution)/shard_map/products/pallas_call | solution.py:86
  95.9 3.0 %products.5 = (bf16[256,512]{1,0:T(8,128)(2,1)S(1)}, bf16[256,512]{1,0:T(8,128)(2,1)S(1)}, bf16[256,512]{1,0:T(8,128)(2,1)S(1)}, bf16[256,512]{1,0:T(8,128)(2,1)...) custom-call(s32[8]{0:T(128)S(1)} %get-tuple-element.69.place, ...), custom_call_target="tpu_custom_call", output_to_operand_aliasing={{6}: (3, {})} | custom-call | flops 1073741824 | bytes 5242880 | tf_op jit(solution)/shard_map/products/pallas_call | solution.py:86
  99.2 12.9 %collective-permute-done = bf16[256,768]{1,0:T(8,128)(2,1)S(1)} collective-permute-done((bf16[256,768]{1,0:T(8,128)(2,1)S(1)}, bf16[256,768]{1,0:T(8,128)(2,1)S(1)}, u32[]{:S(2)}, u32[]{:S(2)}) %collective-permute-start) | collective-permute-done | bytes 393248 | tf_op jit(solution)/shard_map/ppermute | solution.py:179
  112.2 2.1 %collective-permute-start.1 = (bf16[256,768]{1,0:T(8,128)(2,1)S(1)}, bf16[256,768]{1,0:T(8,128)(2,1)S(1)}, u32[]{:S(2)}, u32[]{:S(2)}) collective-permute-start(bf16[256,768]{1,0:T(8,128)(2,1)S(1)} %add_convert_fusion.9), channel_id=1, source_target_pairs={{0,1},{1,2},{2,3},{3,4},{4,5},{5,6},{6,7},{7,0},{8,9},{9,10},{10,1... | collective-permute-start | bytes 1179656 | tf_op jit(solution)/shard_map/ppermute | solution.py:179
  114.4 1.3 collective-permute-start.5
  116.0 1.7 collective-permute-done.15
  117.7 0.4 collective-permute-start.12
  118.2 3.1 %collective-permute-done.19 = bf16[256,512]{1,0:T(8,128)(2,1)S(1)} collective-permute-done((bf16[256,512]{1,0:T(8,128)(2,1)S(1)}, bf16[256,512]{1,0:T(8,128)(2,1)S(1)}, u32[]{:S(2)}, u32[]{:S(2)}) %collective-permute-start.19) | collective-permute-done | bytes 262176 | tf_op jit(solution)/shard_map/ppermute | solution.py:181
  121.4 4.7 %collective-permute-done.1 = bf16[256,768]{1,0:T(8,128)(2,1)S(1)} collective-permute-done((bf16[256,768]{1,0:T(8,128)(2,1)S(1)}, bf16[256,768]{1,0:T(8,128)(2,1)S(1)}, u32[]{:S(2)}, u32[]{:S(2)}) %collective-permute-start.1) | collective-permute-done | bytes 393248 | tf_op jit(solution)/shard_map/ppermute | solution.py:179
  126.2 3.5 %collective-permute-done.5 = bf16[256,768]{1,0:T(8,128)(2,1)S(1)} collective-permute-done((bf16[256,768]{1,0:T(8,128)(2,1)S(1)}, bf16[256,768]{1,0:T(8,128)(2,1)S(1)}, u32[]{:S(2)}, u32[]{:S(2)}) %collective-permute-start.5) | collective-permute-done | bytes 393248 | tf_op jit(solution)/shard_map/ppermute | solution.py:181
  129.9 10.3 %collective-permute-done.16 = bf16[256,512]{1,0:T(8,128)(2,1)S(1)} collective-permute-done((bf16[256,512]{1,0:T(8,128)(2,1)S(1)}, bf16[256,512]{1,0:T(8,128)(2,1)S(1)}, u32[]{:S(2)}, u32[]{:S(2)}) %collective-permute-start.16) | collective-permute-done | bytes 262176 | tf_op jit(solution)/shard_map/ppermute | solution.py:179
  140.3 2.1 %collective-permute-start.17 = (bf16[256,512]{1,0:T(8,128)(2,1)S(1)}, bf16[256,512]{1,0:T(8,128)(2,1)S(1)}, u32[]{:S(2)}, u32[]{:S(2)}) collective-permute-start(bf16[256,512]{1,0:T(8,128)(2,1)S(1)} %add_convert_fusion.12), channel_id=1, source_target_pairs={{0,1},{1,2},{2,3},{3,4},{4,5},{5,6},{6,7},{7,0},{8,9},{9,10},{10,1... | collective-permute-start | bytes 786440 | tf_op jit(solution)/shard_map/ppermute | solution.py:179
  142.5 1.3 collective-permute-start.9
  143.9 4.7 %collective-permute-done.2 = bf16[256,768]{1,0:T(8,128)(2,1)S(1)} collective-permute-done((bf16[256,768]{1,0:T(8,128)(2,1)S(1)}, bf16[256,768]{1,0:T(8,128)(2,1)S(1)}, u32[]{:S(2)}, u32[]{:S(2)}) %collective-permute-start.2) | collective-permute-done | bytes 393248 | tf_op jit(solution)/shard_map/ppermute | solution.py:179
  148.9 10.2 %collective-permute-done.9 = bf16[256,768]{1,0:T(8,128)(2,1)S(1)} collective-permute-done((bf16[256,768]{1,0:T(8,128)(2,1)S(1)}, bf16[256,768]{1,0:T(8,128)(2,1)S(1)}, u32[]{:S(2)}, u32[]{:S(2)}) %collective-permute-start.9) | collective-permute-done | bytes 393248 | tf_op jit(solution)/shard_map/ppermute | solution.py:179
  159.3 3.3 %collective-permute-start.10 = (bf16[256,768]{1,0:T(8,128)(2,1)S(1)}, bf16[256,768]{1,0:T(8,128)(2,1)S(1)}, u32[]{:S(2)}, u32[]{:S(2)}) collective-permute-start(bf16[256,768]{1,0:T(8,128)(2,1)S(1)} %add_convert_fusion.2), channel_id=1, source_target_pairs={{0,7},{1,0},{2,1},{3,2},{4,3},{5,4},{6,5},{7,6},{8,15},{9,8},{10,9... | collective-permute-start | bytes 1179656 | tf_op jit(solution)/shard_map/ppermute | solution.py:179
  162.8 8.0 %collective-permute-done.3 = bf16[256,768]{1,0:T(8,128)(2,1)S(1)} collective-permute-done((bf16[256,768]{1,0:T(8,128)(2,1)S(1)}, bf16[256,768]{1,0:T(8,128)(2,1)S(1)}, u32[]{:S(2)}, u32[]{:S(2)}) %collective-permute-start.3) | collective-permute-done | bytes 393248 | tf_op jit(solution)/shard_map/ppermute | solution.py:179
  170.8 0.4 fusion.5
  171.2 1.1 maximum_bitcast_fusion
  (65 shorter events, 4.2 us)
Async XLA Ops:
  0.6 7.7 %copy-start.4 = (s32[8]{0:T(128)S(1)}, s32[8]{0:T(128)}, u32[]{:S(2)}) copy-start(s32[8]{0:T(128)} %param.11) | copy-start | bytes 100
  0.6 7.7 %copy-start.5 = (s32[32,1]{0,1:T(1,128)S(1)}, s32[32,1]{0,1:T(1,128)}, u32[]{:S(2)}) copy-start(s32[32,1]{0,1:T(1,128)} %param.10) | copy-start | bytes 388
  0.7 33.3 %copy-start.1 = (f32[8,1,16,2048]{3,2,1,0:T(8,128)S(1)}, f32[8,1,16,2048]{3,2,1,0:T(8,128)}, u32[]{:S(2)}) copy-start(f32[8,1,16,2048]{3,2,1,0:T(8,128)} %param.8) | copy-start | bytes 3145732
  0.7 33.3 %all-to-all-start = ((bf16[32,16,2048]{2,1,0:T(8,128)(2,1)}), bf16[32,16,2048]{2,1,0:T(8,128)(2,1)S(1)}, u32[]{:S(2)}, u32[]{:S(2)}) async-start(bf16[32,16,2048]{2,1,0:T(8,128)(2,1)} %bitcast.58), calls=%async_computation | async-start | bytes 4194304 | tf_op jit(solution)/shard_map/all_to_all | solution.py:137
  34.0 1.2 copy-start.2
  38.7 34.0 %all-to-all-start.1 = ((bf16[32,16,2048]{2,1,0:T(8,128)(2,1)}), bf16[32,16,2048]{2,1,0:T(8,128)(2,1)S(1)}, u32[]{:S(2)}, u32[]{:S(2)}) async-start(bf16[32,16,2048]{2,1,0:T(8,128)(2,1)} %bitcast.59), calls=%async_computation.1 | async-start | bytes 4194304 | tf_op jit(solution)/shard_map/all_to_all | solution.py:137
  72.6 2.7 %copy-start = (bf16[1,2048,512]{2,1,0:T(8,128)(2,1)S(1)}, bf16[1,2048,512]{2,1,0:T(8,128)(2,1)}, u32[]{:S(2)}) copy-start(bf16[1,2048,512]{2,1,0:T(8,128)(2,1)} %param.12) | copy-start | bytes 6291460
  76.1 22.9 %collective-permute-start.14 = (bf16[256,512]{1,0:T(8,128)(2,1)S(1)}, bf16[256,512]{1,0:T(8,128)(2,1)S(1)}, u32[]{:S(2)}, u32[]{:S(2)}) collective-permute-start(bf16[256,512]{1,0:T(8,128)(2,1)S(1)} %convolution_convert_fusion.5), channel_id=1, source_target_pairs={{0,1},{1,2},{2,3},{3,4},{4,5},{5,6},{6,7},{7,0},{8,9},{9,10},{10,1... | collective-permute-start | bytes 786440 | tf_op jit(solution)/shard_map/ppermute | solution.py:179
  78.1 21.0 %collective-permute-start.18 = (bf16[256,512]{1,0:T(8,128)(2,1)S(1)}, bf16[256,512]{1,0:T(8,128)(2,1)S(1)}, u32[]{:S(2)}, u32[]{:S(2)}) collective-permute-start(bf16[256,512]{1,0:T(8,128)(2,1)S(1)} %convolution_convert_fusion.4), channel_id=1, source_target_pairs={{0,7},{1,0},{2,1},{3,2},{4,3},{5,4},{6,5},{7,6},{8,15},{9,8},{10,9... | collective-permute-start | bytes 786440 | tf_op jit(solution)/shard_map/ppermute | solution.py:181
  82.9 31.5 %collective-permute-start.7 = (bf16[256,768]{1,0:T(8,128)(2,1)S(1)}, bf16[256,768]{1,0:T(8,128)(2,1)S(1)}, u32[]{:S(2)}, u32[]{:S(2)}) collective-permute-start(bf16[256,768]{1,0:T(8,128)(2,1)S(1)} %convolution_convert_fusion.2), channel_id=1, source_target_pairs={{0,7},{1,0},{2,1},{3,2},{4,3},{5,4},{6,5},{7,6},{8,15},{9,8},{10,9... | collective-permute-start | bytes 1179656 | tf_op jit(solution)/shard_map/ppermute | solution.py:179
  84.9 30.9 %collective-permute-start.11 = (bf16[256,768]{1,0:T(8,128)(2,1)S(1)}, bf16[256,768]{1,0:T(8,128)(2,1)S(1)}, u32[]{:S(2)}, u32[]{:S(2)}) collective-permute-start(bf16[256,768]{1,0:T(8,128)(2,1)S(1)} %convolution_convert_fusion), channel_id=1, source_target_pairs={{0,1},{1,2},{2,3},{3,4},{4,5},{5,6},{6,7},{7,0},{8,9},{9,10},{10,1... | collective-permute-start | bytes 1179656 | tf_op jit(solution)/shard_map/ppermute | solution.py:181
  85.0 27.2 %collective-permute-start.4 = (bf16[256,768]{1,0:T(8,128)(2,1)S(1)}, bf16[256,768]{1,0:T(8,128)(2,1)S(1)}, u32[]{:S(2)}, u32[]{:S(2)}) collective-permute-start(bf16[256,768]{1,0:T(8,128)(2,1)S(1)} %convolution_convert_fusion.1), channel_id=1, source_target_pairs={{0,7},{1,0},{2,1},{3,2},{4,3},{5,4},{6,5},{7,6},{8,15},{9,8},{10,9... | collective-permute-start | bytes 1179656 | tf_op jit(solution)/shard_map/ppermute | solution.py:181
  99.0 13.1 %collective-permute-start = (bf16[256,768]{1,0:T(8,128)(2,1)S(1)}, bf16[256,768]{1,0:T(8,128)(2,1)S(1)}, u32[]{:S(2)}, u32[]{:S(2)}) collective-permute-start(bf16[256,768]{1,0:T(8,128)(2,1)S(1)} %convolution_convert_fusion.3), channel_id=1, source_target_pairs={{0,1},{1,2},{2,3},{3,4},{4,5},{5,6},{6,7},{7,0},{8,9},{9,10},{10,1... | collective-permute-start | bytes 1179656 | tf_op jit(solution)/shard_map/ppermute | solution.py:179
  99.1 18.6 %collective-permute-start.15 = (bf16[256,512]{1,0:T(8,128)(2,1)S(1)}, bf16[256,512]{1,0:T(8,128)(2,1)S(1)}, u32[]{:S(2)}, u32[]{:S(2)}) collective-permute-start(bf16[256,512]{1,0:T(8,128)(2,1)S(1)} %add_convert_fusion.14), channel_id=1, source_target_pairs={{0,1},{1,2},{2,3},{3,4},{4,5},{5,6},{6,7},{7,0},{8,9},{9,10},{10,1... | collective-permute-start | bytes 786440 | tf_op jit(solution)/shard_map/ppermute | solution.py:179
  112.1 9.2 %collective-permute-start.19 = (bf16[256,512]{1,0:T(8,128)(2,1)S(1)}, bf16[256,512]{1,0:T(8,128)(2,1)S(1)}, u32[]{:S(2)}, u32[]{:S(2)}) collective-permute-start(bf16[256,512]{1,0:T(8,128)(2,1)S(1)} %add_convert_fusion.11), channel_id=1, source_target_pairs={{0,7},{1,0},{2,1},{3,2},{4,3},{5,4},{6,5},{7,6},{8,15},{9,8},{10,9... | collective-permute-start | bytes 786440 | tf_op jit(solution)/shard_map/ppermute | solution.py:181
  112.2 13.9 %collective-permute-start.1 = (bf16[256,768]{1,0:T(8,128)(2,1)S(1)}, bf16[256,768]{1,0:T(8,128)(2,1)S(1)}, u32[]{:S(2)}, u32[]{:S(2)}) collective-permute-start(bf16[256,768]{1,0:T(8,128)(2,1)S(1)} %add_convert_fusion.9), channel_id=1, source_target_pairs={{0,1},{1,2},{2,3},{3,4},{4,5},{5,6},{6,7},{7,0},{8,9},{9,10},{10,1... | collective-permute-start | bytes 1179656 | tf_op jit(solution)/shard_map/ppermute | solution.py:179
  114.4 15.3 %collective-permute-start.5 = (bf16[256,768]{1,0:T(8,128)(2,1)S(1)}, bf16[256,768]{1,0:T(8,128)(2,1)S(1)}, u32[]{:S(2)}, u32[]{:S(2)}) collective-permute-start(bf16[256,768]{1,0:T(8,128)(2,1)S(1)} %add_convert_fusion.6), channel_id=1, source_target_pairs={{0,7},{1,0},{2,1},{3,2},{4,3},{5,4},{6,5},{7,6},{8,15},{9,8},{10,9... | collective-permute-start | bytes 1179656 | tf_op jit(solution)/shard_map/ppermute | solution.py:181
  115.8 24.4 %collective-permute-start.8 = (bf16[256,768]{1,0:T(8,128)(2,1)S(1)}, bf16[256,768]{1,0:T(8,128)(2,1)S(1)}, u32[]{:S(2)}, u32[]{:S(2)}) collective-permute-start(bf16[256,768]{1,0:T(8,128)(2,1)S(1)} %add_convert_fusion.4), channel_id=1, source_target_pairs={{0,7},{1,0},{2,1},{3,2},{4,3},{5,4},{6,5},{7,6},{8,15},{9,8},{10,9... | collective-permute-start | bytes 1179656 | tf_op jit(solution)/shard_map/ppermute | solution.py:179
  117.7 24.8 %collective-permute-start.12 = (bf16[256,768]{1,0:T(8,128)(2,1)S(1)}, bf16[256,768]{1,0:T(8,128)(2,1)S(1)}, u32[]{:S(2)}, u32[]{:S(2)}) collective-permute-start(bf16[256,768]{1,0:T(8,128)(2,1)S(1)} %add_convert_fusion.1), channel_id=1, source_target_pairs={{0,1},{1,2},{2,3},{3,4},{4,5},{5,6},{6,7},{7,0},{8,9},{9,10},{10,1... | collective-permute-start | bytes 1179656 | tf_op jit(solution)/shard_map/ppermute | solution.py:181
  121.3 18.9 %collective-permute-start.16 = (bf16[256,512]{1,0:T(8,128)(2,1)S(1)}, bf16[256,512]{1,0:T(8,128)(2,1)S(1)}, u32[]{:S(2)}, u32[]{:S(2)}) collective-permute-start(bf16[256,512]{1,0:T(8,128)(2,1)S(1)} %add_convert_fusion.13), channel_id=1, source_target_pairs={{0,1},{1,2},{2,3},{3,4},{4,5},{5,6},{6,7},{7,0},{8,9},{9,10},{10,1... | collective-permute-start | bytes 786440 | tf_op jit(solution)/shard_map/ppermute | solution.py:179
  126.1 33.1 %collective-permute-start.20 = (bf16[256,512]{1,0:T(8,128)(2,1)S(1)}, bf16[256,512]{1,0:T(8,128)(2,1)S(1)}, u32[]{:S(2)}, u32[]{:S(2)}) collective-permute-start(bf16[256,512]{1,0:T(8,128)(2,1)S(1)} %add_convert_fusion.10), channel_id=1, source_target_pairs={{0,7},{1,0},{2,1},{3,2},{4,3},{5,4},{6,5},{7,6},{8,15},{9,8},{10,9... | collective-permute-start | bytes 786440 | tf_op jit(solution)/shard_map/ppermute | solution.py:181
  129.8 18.9 %collective-permute-start.2 = (bf16[256,768]{1,0:T(8,128)(2,1)S(1)}, bf16[256,768]{1,0:T(8,128)(2,1)S(1)}, u32[]{:S(2)}, u32[]{:S(2)}) collective-permute-start(bf16[256,768]{1,0:T(8,128)(2,1)S(1)} %add_convert_fusion.8), channel_id=1, source_target_pairs={{0,1},{1,2},{2,3},{3,4},{4,5},{5,6},{6,7},{7,0},{8,9},{9,10},{10,1... | collective-permute-start | bytes 1179656 | tf_op jit(solution)/shard_map/ppermute | solution.py:179
  140.2 22.6 %collective-permute-start.6 = (bf16[256,768]{1,0:T(8,128)(2,1)S(1)}, bf16[256,768]{1,0:T(8,128)(2,1)S(1)}, u32[]{:S(2)}, u32[]{:S(2)}) collective-permute-start(bf16[256,768]{1,0:T(8,128)(2,1)S(1)} %add_convert_fusion.5), channel_id=1, source_target_pairs={{0,7},{1,0},{2,1},{3,2},{4,3},{5,4},{6,5},{7,6},{8,15},{9,8},{10,9... | collective-permute-start | bytes 1179656 | tf_op jit(solution)/shard_map/ppermute | solution.py:181
  140.3 22.3 %collective-permute-start.17 = (bf16[256,512]{1,0:T(8,128)(2,1)S(1)}, bf16[256,512]{1,0:T(8,128)(2,1)S(1)}, u32[]{:S(2)}, u32[]{:S(2)}) collective-permute-start(bf16[256,512]{1,0:T(8,128)(2,1)S(1)} %add_convert_fusion.12), channel_id=1, source_target_pairs={{0,1},{1,2},{2,3},{3,4},{4,5},{5,6},{6,7},{7,0},{8,9},{9,10},{10,1... | collective-permute-start | bytes 786440 | tf_op jit(solution)/shard_map/ppermute | solution.py:179
  142.4 20.2 %copy-start.3 = (bf16[1,256,2048]{2,1,0:T(8,128)(2,1)S(1)}, bf16[1,256,2048]{2,1,0:T(8,128)(2,1)}, u32[]{:S(2)}) copy-start(bf16[1,256,2048]{2,1,0:T(8,128)(2,1)} %param.13) | copy-start | bytes 3145732
  142.5 16.7 %collective-permute-start.9 = (bf16[256,768]{1,0:T(8,128)(2,1)S(1)}, bf16[256,768]{1,0:T(8,128)(2,1)S(1)}, u32[]{:S(2)}, u32[]{:S(2)}) collective-permute-start(bf16[256,768]{1,0:T(8,128)(2,1)S(1)} %add_convert_fusion.3), channel_id=1, source_target_pairs={{0,7},{1,0},{2,1},{3,2},{4,3},{5,4},{6,5},{7,6},{8,15},{9,8},{10,9... | collective-permute-start | bytes 1179656 | tf_op jit(solution)/shard_map/ppermute | solution.py:179
  148.6 14.1 %collective-permute-start.13 = (bf16[256,768]{1,0:T(8,128)(2,1)S(1)}, bf16[256,768]{1,0:T(8,128)(2,1)S(1)}, u32[]{:S(2)}, u32[]{:S(2)}) collective-permute-start(bf16[256,768]{1,0:T(8,128)(2,1)S(1)} %add_convert_fusion), channel_id=1, source_target_pairs={{0,1},{1,2},{2,3},{3,4},{4,5},{5,6},{6,7},{7,0},{8,9},{9,10},{10,1... | collective-permute-start | bytes 1179656 | tf_op jit(solution)/shard_map/ppermute | solution.py:181
  159.2 11.6 %collective-permute-start.3 = (bf16[256,768]{1,0:T(8,128)(2,1)S(1)}, bf16[256,768]{1,0:T(8,128)(2,1)S(1)}, u32[]{:S(2)}, u32[]{:S(2)}) collective-permute-start(bf16[256,768]{1,0:T(8,128)(2,1)S(1)} %add_convert_fusion.7), channel_id=1, source_target_pairs={{0,1},{1,2},{2,3},{3,4},{4,5},{5,6},{6,7},{7,0},{8,9},{9,10},{10,1... | collective-permute-start | bytes 1179656 | tf_op jit(solution)/shard_map/ppermute | solution.py:179
  159.3 11.5 %collective-permute-start.10 = (bf16[256,768]{1,0:T(8,128)(2,1)S(1)}, bf16[256,768]{1,0:T(8,128)(2,1)S(1)}, u32[]{:S(2)}, u32[]{:S(2)}) collective-permute-start(bf16[256,768]{1,0:T(8,128)(2,1)S(1)} %add_convert_fusion.2), channel_id=1, source_target_pairs={{0,7},{1,0},{2,1},{3,2},{4,3},{5,4},{6,5},{7,6},{8,15},{9,8},{10,9... | collective-permute-start | bytes 1179656 | tf_op jit(solution)/shard_map/ppermute | solution.py:179

commit v3 on v2

--- a/solution.py
+++ b/solution.py
@@ -111,6 +111,37 @@
     return list(outs[:-1]), outs[-1]
 
 
+def finish_kernel(resid, *refs):
+    ends, out = refs[:-1], refs[-1]
+    at = 0
+    for own, ahead, behind in zip(ends[0::3], ends[1::3], ends[2::3]):
+        here = slice(at, at + own.shape[1])
+        total = own[...].astype(jnp.float32) + resid[:, here].astype(jnp.float32)
+        total = total + ahead[...].astype(jnp.float32) + behind[...].astype(jnp.float32)
+        out[:, here] = total.astype(jnp.bfloat16)
+        at += own.shape[1]
+
+
+def finish(resid, ends):
+    tokens, width = resid.shape
+    half = tokens // 2
+    rows = lambda i: (i, 0)
+    arrays = [value for end in ends for value in end]
+    return pl.pallas_call(
+        finish_kernel,
+        grid=(2,),
+        in_specs=[pl.BlockSpec((half, width), rows)]
+        + [pl.BlockSpec((half, value.shape[1]), rows) for value in arrays],
+        out_specs=pl.BlockSpec((half, width), rows),
+        out_shape=jax.ShapeDtypeStruct((tokens, width), jnp.bfloat16),
+        compiler_params=pltpu.CompilerParams(vmem_limit_bytes=LIMIT * 1024 * 1024),
+        cost_estimate=pl.CostEstimate(
+            flops=3 * resid.size, bytes_accessed=10 * resid.size, transcendentals=0
+        ),
+        name="finish",
+    )(resid, *arrays)
+
+
 def body(trained, outer_params, momentum, path_module, module_slot, hidden, residual):
     paths = lax.axis_size("path")
     shards = lax.axis_size("shard")
@@ -183,11 +214,7 @@
                     ahead = add(parts[k], ahead)
                 if k > 1:
                     behind = add(parts[shards + 1 - k], behind)
-            own = parts[0].astype(jnp.float32)
-            own = own + residual[0, :, self.lo:self.lo + self.w].astype(jnp.float32)
-            self.total = (own + ahead.astype(jnp.float32) + behind.astype(jnp.float32)).astype(
-                jnp.bfloat16
-            )
+            self.ends = (parts[0], ahead, behind)
             return [whole]
 
     rings, lo = [], 0
@@ -198,12 +225,12 @@
     whole = []
     for r in rings:
         whole = r.run(later, whole)
-    mixed = [r.total for r in rings]
+    mixed = finish(residual[0], [r.ends for r in rings])
     return (
         params.reshape(outer_params.shape),
         moments.reshape(outer_params.shape),
         whole[0][None],
-        jnp.concatenate(mixed, axis=1)[None],
+        mixed[None],
     )
 
 

time: 173 us -> 177 us (1.023)
  waiting for transfers between devices: 110 us -> 117 us
  starting transfers between devices: 38.3 us -> 36 us
    ppermute x12, waiting for transfers between devices: 52.6 us -> 59.9 us  [run(): ahead = lax.ppermute(ahead, 'shard', self.one)]
    ppermute x12, starting transfers between devices: 13 us -> 9.76 us  [run(): ahead = lax.ppermute(ahead, 'shard', self.one)]
where the time goes in v3:
time: 177 us
  waiting for transfers between devices  117 us (66%)
  starting transfers between devices  36 us (20%)
  Pallas kernels  15.7 us (9%)
  matrix products  4.18 us (2%)
    ppermute x12, waiting for transfers between devices, run(): ahead = lax.ppermute(ahead, 'shard', self.one)  59.9 us
    all_to_all x2, waiting for transfers between devices, exchange(): lax.all_to_all(block.reshape(paths, piece, w), 'path', split_axis=0, conc...  50.4 us
    all_to_all x2, starting transfers between devices, exchange(): lax.all_to_all(block.reshape(paths, piece, w), 'path', split_axis=0, conc...  16.1 us
    pallas_call x3, Pallas kernels, products(): pl.pallas_call(product_kernel, grid_spec=pltpu.PrefetchScalarGridSpec(num...  10.8 us
    ppermute x9, starting transfers between devices, run(): behind = lax.ppermute(behind, 'shard', self.other)  10.1 us
    ppermute x12, starting transfers between devices, run(): ahead = lax.ppermute(ahead, 'shard', self.one)  9.76 us
    ppermute x9, waiting for transfers between devices, run(): behind = lax.ppermute(behind, 'shard', self.other)  6.69 us
    dot_general x6, matrix products, head(): jnp.dot(block, slab[:, self.lo:self.lo + self.w], preferred_element_type=...  4.18 us
  transfers between devices with their start and end apart: 23, of which 11 were waited for; matrix products, arithmetic and copies ran while one was open for 2% of the time, Pallas kernels for 6%

profile of v3, /device:TPU:6, one launch (start us, length us, event | category | flops | bytes accessed | tf_op | source)
XLA Modules:
  0.0 177.0 jit_solution(11746717930929598314)
XLA Ops:
  0.7 7.7 %all-to-all-start = ((bf16[32,16,2048]{2,1,0:T(8,128)(2,1)}), bf16[32,16,2048]{2,1,0:T(8,128)(2,1)S(1)}, u32[]{:S(2)}, u32[]{:S(2)}) async-start(bf16[32,16,2048]{2,1,0:T(8,128)(2,1)} %bitcast.50), calls=%async_computation | async-start | bytes 4194304 | tf_op jit(solution)/shard_map/all_to_all | solution.py:168
  9.1 24.8 %all-to-all-done = bf16[32,16,2048]{2,1,0:T(8,128)(2,1)S(1)} async-done(((bf16[32,16,2048]{2,1,0:T(8,128)(2,1)}), bf16[32,16,2048]{2,1,0:T(8,128)(2,1)S(1)}, u32[]{:S(2)}, u32[]{:S(2)}) %all-to-all-start) | async-done | bytes 2097184 | tf_op jit(solution)/shard_map/all_to_all | solution.py:168
  34.0 1.2 copy-done.2
  35.2 3.5 %update.1 = (f32[128,2048]{1,0:T(8,128)}, f32[128,2048]{1,0:T(8,128)}, bf16[512,2048]{1,0:T(8,128)(2,1)}) custom-call(bf16[128,512]{1,0:T(8,128)(2,1)S(1)} %fusion.14.pick, bf16[512,128]{1,0:T(8,128)(2,1)S(1)} %fusion.15.back, f32[128,1]{1,0:T(8,128)S(1)} %broadcast_in_dim_reshape.4.count, bf16[512,2048]{1,0:T(8,128)(2,1)S(1)} %bitcast.45, ...), custom_call_target="tpu_custom_call" | custom-call | flops 536870912 | bytes 8388608 | tf_op jit(solution)/shard_map/update/pallas_call | solution.py:36
  38.7 8.4 %all-to-all-start.1 = ((bf16[32,16,2048]{2,1,0:T(8,128)(2,1)}), bf16[32,16,2048]{2,1,0:T(8,128)(2,1)S(1)}, u32[]{:S(2)}, u32[]{:S(2)}) async-start(bf16[32,16,2048]{2,1,0:T(8,128)(2,1)} %bitcast.51), calls=%async_computation.1 | async-start | bytes 4194304 | tf_op jit(solution)/shard_map/all_to_all | solution.py:168
  47.1 25.5 %all-to-all-done.1 = bf16[32,16,2048]{2,1,0:T(8,128)(2,1)S(1)} async-done(((bf16[32,16,2048]{2,1,0:T(8,128)(2,1)}), bf16[32,16,2048]{2,1,0:T(8,128)(2,1)S(1)}, u32[]{:S(2)}, u32[]{:S(2)}) %all-to-all-start.1) | async-done | bytes 2097184 | tf_op jit(solution)/shard_map/all_to_all | solution.py:168
  72.7 1.4 convolution_convert_fusion.5
  74.1 1.3 convolution_convert_fusion.3
  75.7 0.4 convolution_convert_fusion.1
  76.1 2.0 %collective-permute-start.14 = (bf16[256,512]{1,0:T(8,128)(2,1)S(1)}, bf16[256,512]{1,0:T(8,128)(2,1)S(1)}, u32[]{:S(2)}, u32[]{:S(2)}) collective-permute-start(bf16[256,512]{1,0:T(8,128)(2,1)S(1)} %convolution_convert_fusion.5), channel_id=1, source_target_pairs={{0,1},{1,2},{2,3},{3,4},{4,5},{5,6},{6,7},{7,0},{8,9},{9,10},{10,1... | collective-permute-start | bytes 786440 | tf_op jit(solution)/shard_map/ppermute | solution.py:210
  78.1 4.0 %collective-permute-start.18 = (bf16[256,512]{1,0:T(8,128)(2,1)S(1)}, bf16[256,512]{1,0:T(8,128)(2,1)S(1)}, u32[]{:S(2)}, u32[]{:S(2)}) collective-permute-start(bf16[256,512]{1,0:T(8,128)(2,1)S(1)} %convolution_convert_fusion.4), channel_id=1, source_target_pairs={{0,7},{1,0},{2,1},{3,2},{4,3},{5,4},{6,5},{7,6},{8,15},{9,8},{10,9... | collective-permute-start | bytes 786440 | tf_op jit(solution)/shard_map/ppermute | solution.py:212
  82.5 0.4 convolution_convert_fusion.2
  82.9 2.0 %collective-permute-start.7 = (bf16[256,768]{1,0:T(8,128)(2,1)S(1)}, bf16[256,768]{1,0:T(8,128)(2,1)S(1)}, u32[]{:S(2)}, u32[]{:S(2)}) collective-permute-start(bf16[256,768]{1,0:T(8,128)(2,1)S(1)} %convolution_convert_fusion.2), channel_id=1, source_target_pairs={{0,7},{1,0},{2,1},{3,2},{4,3},{5,4},{6,5},{7,6},{8,15},{9,8},{10,9... | collective-permute-start | bytes 1179656 | tf_op jit(solution)/shard_map/ppermute | solution.py:210
  85.0 3.1 %collective-permute-start.4 = (bf16[256,768]{1,0:T(8,128)(2,1)S(1)}, bf16[256,768]{1,0:T(8,128)(2,1)S(1)}, u32[]{:S(2)}, u32[]{:S(2)}) collective-permute-start(bf16[256,768]{1,0:T(8,128)(2,1)S(1)} %convolution_convert_fusion.1), channel_id=1, source_target_pairs={{0,7},{1,0},{2,1},{3,2},{4,3},{5,4},{6,5},{7,6},{8,15},{9,8},{10,9... | collective-permute-start | bytes 1179656 | tf_op jit(solution)/shard_map/ppermute | solution.py:212
  88.2 3.9 %products.3 = (bf16[256,768]{1,0:T(8,128)(2,1)S(1)}, bf16[256,768]{1,0:T(8,128)(2,1)S(1)}, bf16[256,768]{1,0:T(8,128)(2,1)S(1)}, bf16[256,768]{1,0:T(8,128)(2,1)...) custom-call(s32[8]{0:T(128)S(1)} %get-tuple-element.67.place, ...), custom_call_target="tpu_custom_call" | custom-call | flops 1610612736 | bytes 6815744 | tf_op jit(solution)/shard_map/products/pallas_call | solution.py:86
  92.0 3.9 %products.4 = (bf16[256,768]{1,0:T(8,128)(2,1)S(1)}, bf16[256,768]{1,0:T(8,128)(2,1)S(1)}, bf16[256,768]{1,0:T(8,128)(2,1)S(1)}, bf16[256,768]{1,0:T(8,128)(2,1)...) custom-call(s32[8]{0:T(128)S(1)} %get-tuple-element.66.place, ...), custom_call_target="tpu_custom_call", output_to_operand_aliasing={{6}: (3, {})} | custom-call | flops 1610612736 | bytes 6815744 | tf_op jit(solution)/shard_map/products/pallas_call | solution.py:86
  95.9 3.0 %products.5 = (bf16[256,512]{1,0:T(8,128)(2,1)S(1)}, bf16[256,512]{1,0:T(8,128)(2,1)S(1)}, bf16[256,512]{1,0:T(8,128)(2,1)S(1)}, bf16[256,512]{1,0:T(8,128)(2,1)...) custom-call(s32[8]{0:T(128)S(1)} %get-tuple-element.67.place, ...), custom_call_target="tpu_custom_call", output_to_operand_aliasing={{6}: (3, {})} | custom-call | flops 1073741824 | bytes 5242880 | tf_op jit(solution)/shard_map/products/pallas_call | solution.py:86
  99.2 12.9 %collective-permute-done = bf16[256,768]{1,0:T(8,128)(2,1)S(1)} collective-permute-done((bf16[256,768]{1,0:T(8,128)(2,1)S(1)}, bf16[256,768]{1,0:T(8,128)(2,1)S(1)}, u32[]{:S(2)}, u32[]{:S(2)}) %collective-permute-start) | collective-permute-done | bytes 393248 | tf_op jit(solution)/shard_map/ppermute | solution.py:210
  112.2 2.1 %collective-permute-start.1 = (bf16[256,768]{1,0:T(8,128)(2,1)S(1)}, bf16[256,768]{1,0:T(8,128)(2,1)S(1)}, u32[]{:S(2)}, u32[]{:S(2)}) collective-permute-start(bf16[256,768]{1,0:T(8,128)(2,1)S(1)} %add_convert_fusion.9), channel_id=1, source_target_pairs={{0,1},{1,2},{2,3},{3,4},{4,5},{5,6},{6,7},{7,0},{8,9},{9,10},{10,1... | collective-permute-start | bytes 1179656 | tf_op jit(solution)/shard_map/ppermute | solution.py:210
  114.4 1.3 collective-permute-start.5
  116.0 1.7 collective-permute-done.15
  117.7 0.4 collective-permute-start.12
  118.2 3.2 %collective-permute-done.19 = bf16[256,512]{1,0:T(8,128)(2,1)S(1)} collective-permute-done((bf16[256,512]{1,0:T(8,128)(2,1)S(1)}, bf16[256,512]{1,0:T(8,128)(2,1)S(1)}, u32[]{:S(2)}, u32[]{:S(2)}) %collective-permute-start.19) | collective-permute-done | bytes 262176 | tf_op jit(solution)/shard_map/ppermute | solution.py:212
  121.4 4.7 %collective-permute-done.1 = bf16[256,768]{1,0:T(8,128)(2,1)S(1)} collective-permute-done((bf16[256,768]{1,0:T(8,128)(2,1)S(1)}, bf16[256,768]{1,0:T(8,128)(2,1)S(1)}, u32[]{:S(2)}, u32[]{:S(2)}) %collective-permute-start.1) | collective-permute-done | bytes 393248 | tf_op jit(solution)/shard_map/ppermute | solution.py:210
  126.2 3.5 %collective-permute-done.5 = bf16[256,768]{1,0:T(8,128)(2,1)S(1)} collective-permute-done((bf16[256,768]{1,0:T(8,128)(2,1)S(1)}, bf16[256,768]{1,0:T(8,128)(2,1)S(1)}, u32[]{:S(2)}, u32[]{:S(2)}) %collective-permute-start.5) | collective-permute-done | bytes 393248 | tf_op jit(solution)/shard_map/ppermute | solution.py:212
  129.9 8.3 %collective-permute-done.8 = bf16[256,768]{1,0:T(8,128)(2,1)S(1)} collective-permute-done((bf16[256,768]{1,0:T(8,128)(2,1)S(1)}, bf16[256,768]{1,0:T(8,128)(2,1)S(1)}, u32[]{:S(2)}, u32[]{:S(2)}) %collective-permute-start.8) | collective-permute-done | bytes 393248 | tf_op jit(solution)/shard_map/ppermute | solution.py:210
  138.2 1.2 collective-permute-start.6
  139.7 8.7 %collective-permute-done.2 = bf16[256,768]{1,0:T(8,128)(2,1)S(1)} collective-permute-done((bf16[256,768]{1,0:T(8,128)(2,1)S(1)}, bf16[256,768]{1,0:T(8,128)(2,1)S(1)}, u32[]{:S(2)}, u32[]{:S(2)}) %collective-permute-start.2) | collective-permute-done | bytes 393248 | tf_op jit(solution)/shard_map/ppermute | solution.py:210
  148.4 10.7 %collective-permute-done.9 = bf16[256,768]{1,0:T(8,128)(2,1)S(1)} collective-permute-done((bf16[256,768]{1,0:T(8,128)(2,1)S(1)}, bf16[256,768]{1,0:T(8,128)(2,1)S(1)}, u32[]{:S(2)}, u32[]{:S(2)}) %collective-permute-start.9) | collective-permute-done | bytes 393248 | tf_op jit(solution)/shard_map/ppermute | solution.py:210
  159.3 3.3 %collective-permute-start.10 = (bf16[256,768]{1,0:T(8,128)(2,1)S(1)}, bf16[256,768]{1,0:T(8,128)(2,1)S(1)}, u32[]{:S(2)}, u32[]{:S(2)}) collective-permute-start(bf16[256,768]{1,0:T(8,128)(2,1)S(1)} %add_convert_fusion.2), channel_id=1, source_target_pairs={{0,7},{1,0},{2,1},{3,2},{4,3},{5,4},{6,5},{7,6},{8,15},{9,8},{10,9... | collective-permute-start | bytes 1179656 | tf_op jit(solution)/shard_map/ppermute | solution.py:210
  162.8 12.9 %collective-permute-done.17.refs_7_ = bf16[256,512]{1,0:T(8,128)(2,1)S(1)} collective-permute-done((bf16[256,512]{1,0:T(8,128)(2,1)S(1)}, bf16[256,512]{1,0:T(8,128)(2,1)S(1)}, u32[]{:S(2)}, u32[]{:S(2)}) %collective-permute-start.17) | collective-permute-done | bytes 262176 | tf_op jit(solution)/shard_map/ppermute | solution.py:210
  175.7 1.4 finish.1
  (63 shorter events, 3.2 us)
Async XLA Ops:
  0.6 7.7 %copy-start.4 = (s32[8]{0:T(128)S(1)}, s32[8]{0:T(128)}, u32[]{:S(2)}) copy-start(s32[8]{0:T(128)} %param.11) | copy-start | bytes 100
  0.6 7.7 %copy-start.5 = (s32[32,1]{0,1:T(1,128)S(1)}, s32[32,1]{0,1:T(1,128)}, u32[]{:S(2)}) copy-start(s32[32,1]{0,1:T(1,128)} %param.10) | copy-start | bytes 388
  0.7 33.3 %copy-start.1 = (f32[8,1,16,2048]{3,2,1,0:T(8,128)S(1)}, f32[8,1,16,2048]{3,2,1,0:T(8,128)}, u32[]{:S(2)}) copy-start(f32[8,1,16,2048]{3,2,1,0:T(8,128)} %param.8) | copy-start | bytes 3145732
  0.7 33.3 %all-to-all-start = ((bf16[32,16,2048]{2,1,0:T(8,128)(2,1)}), bf16[32,16,2048]{2,1,0:T(8,128)(2,1)S(1)}, u32[]{:S(2)}, u32[]{:S(2)}) async-start(bf16[32,16,2048]{2,1,0:T(8,128)(2,1)} %bitcast.50), calls=%async_computation | async-start | bytes 4194304 | tf_op jit(solution)/shard_map/all_to_all | solution.py:168
  34.0 1.2 copy-start.2
  38.7 34.0 %all-to-all-start.1 = ((bf16[32,16,2048]{2,1,0:T(8,128)(2,1)}), bf16[32,16,2048]{2,1,0:T(8,128)(2,1)S(1)}, u32[]{:S(2)}, u32[]{:S(2)}) async-start(bf16[32,16,2048]{2,1,0:T(8,128)(2,1)} %bitcast.51), calls=%async_computation.1 | async-start | bytes 4194304 | tf_op jit(solution)/shard_map/all_to_all | solution.py:168
  72.6 2.7 %copy-start = (bf16[1,2048,512]{2,1,0:T(8,128)(2,1)S(1)}, bf16[1,2048,512]{2,1,0:T(8,128)(2,1)}, u32[]{:S(2)}) copy-start(bf16[1,2048,512]{2,1,0:T(8,128)(2,1)} %param.12) | copy-start | bytes 6291460
  76.1 22.9 %collective-permute-start.14 = (bf16[256,512]{1,0:T(8,128)(2,1)S(1)}, bf16[256,512]{1,0:T(8,128)(2,1)S(1)}, u32[]{:S(2)}, u32[]{:S(2)}) collective-permute-start(bf16[256,512]{1,0:T(8,128)(2,1)S(1)} %convolution_convert_fusion.5), channel_id=1, source_target_pairs={{0,1},{1,2},{2,3},{3,4},{4,5},{5,6},{6,7},{7,0},{8,9},{9,10},{10,1... | collective-permute-start | bytes 786440 | tf_op jit(solution)/shard_map/ppermute | solution.py:210
  78.1 21.0 %collective-permute-start.18 = (bf16[256,512]{1,0:T(8,128)(2,1)S(1)}, bf16[256,512]{1,0:T(8,128)(2,1)S(1)}, u32[]{:S(2)}, u32[]{:S(2)}) collective-permute-start(bf16[256,512]{1,0:T(8,128)(2,1)S(1)} %convolution_convert_fusion.4), channel_id=1, source_target_pairs={{0,7},{1,0},{2,1},{3,2},{4,3},{5,4},{6,5},{7,6},{8,15},{9,8},{10,9... | collective-permute-start | bytes 786440 | tf_op jit(solution)/shard_map/ppermute | solution.py:212
  82.9 31.5 %collective-permute-start.7 = (bf16[256,768]{1,0:T(8,128)(2,1)S(1)}, bf16[256,768]{1,0:T(8,128)(2,1)S(1)}, u32[]{:S(2)}, u32[]{:S(2)}) collective-permute-start(bf16[256,768]{1,0:T(8,128)(2,1)S(1)} %convolution_convert_fusion.2), channel_id=1, source_target_pairs={{0,7},{1,0},{2,1},{3,2},{4,3},{5,4},{6,5},{7,6},{8,15},{9,8},{10,9... | collective-permute-start | bytes 1179656 | tf_op jit(solution)/shard_map/ppermute | solution.py:210
  84.9 30.9 %collective-permute-start.11 = (bf16[256,768]{1,0:T(8,128)(2,1)S(1)}, bf16[256,768]{1,0:T(8,128)(2,1)S(1)}, u32[]{:S(2)}, u32[]{:S(2)}) collective-permute-start(bf16[256,768]{1,0:T(8,128)(2,1)S(1)} %convolution_convert_fusion), channel_id=1, source_target_pairs={{0,1},{1,2},{2,3},{3,4},{4,5},{5,6},{6,7},{7,0},{8,9},{9,10},{10,1... | collective-permute-start | bytes 1179656 | tf_op jit(solution)/shard_map/ppermute | solution.py:212
  85.0 27.2 %collective-permute-start.4 = (bf16[256,768]{1,0:T(8,128)(2,1)S(1)}, bf16[256,768]{1,0:T(8,128)(2,1)S(1)}, u32[]{:S(2)}, u32[]{:S(2)}) collective-permute-start(bf16[256,768]{1,0:T(8,128)(2,1)S(1)} %convolution_convert_fusion.1), channel_id=1, source_target_pairs={{0,7},{1,0},{2,1},{3,2},{4,3},{5,4},{6,5},{7,6},{8,15},{9,8},{10,9... | collective-permute-start | bytes 1179656 | tf_op jit(solution)/shard_map/ppermute | solution.py:212
  99.0 13.1 %collective-permute-start = (bf16[256,768]{1,0:T(8,128)(2,1)S(1)}, bf16[256,768]{1,0:T(8,128)(2,1)S(1)}, u32[]{:S(2)}, u32[]{:S(2)}) collective-permute-start(bf16[256,768]{1,0:T(8,128)(2,1)S(1)} %convolution_convert_fusion.3), channel_id=1, source_target_pairs={{0,1},{1,2},{2,3},{3,4},{4,5},{5,6},{6,7},{7,0},{8,9},{9,10},{10,1... | collective-permute-start | bytes 1179656 | tf_op jit(solution)/shard_map/ppermute | solution.py:210
  99.1 18.6 %collective-permute-start.15 = (bf16[256,512]{1,0:T(8,128)(2,1)S(1)}, bf16[256,512]{1,0:T(8,128)(2,1)S(1)}, u32[]{:S(2)}, u32[]{:S(2)}) collective-permute-start(bf16[256,512]{1,0:T(8,128)(2,1)S(1)} %add_convert_fusion.14), channel_id=1, source_target_pairs={{0,1},{1,2},{2,3},{3,4},{4,5},{5,6},{6,7},{7,0},{8,9},{9,10},{10,1... | collective-permute-start | bytes 786440 | tf_op jit(solution)/shard_map/ppermute | solution.py:210
  112.1 9.2 %collective-permute-start.19 = (bf16[256,512]{1,0:T(8,128)(2,1)S(1)}, bf16[256,512]{1,0:T(8,128)(2,1)S(1)}, u32[]{:S(2)}, u32[]{:S(2)}) collective-permute-start(bf16[256,512]{1,0:T(8,128)(2,1)S(1)} %add_convert_fusion.11), channel_id=1, source_target_pairs={{0,7},{1,0},{2,1},{3,2},{4,3},{5,4},{6,5},{7,6},{8,15},{9,8},{10,9... | collective-permute-start | bytes 786440 | tf_op jit(solution)/shard_map/ppermute | solution.py:212
  112.2 13.9 %collective-permute-start.1 = (bf16[256,768]{1,0:T(8,128)(2,1)S(1)}, bf16[256,768]{1,0:T(8,128)(2,1)S(1)}, u32[]{:S(2)}, u32[]{:S(2)}) collective-permute-start(bf16[256,768]{1,0:T(8,128)(2,1)S(1)} %add_convert_fusion.9), channel_id=1, source_target_pairs={{0,1},{1,2},{2,3},{3,4},{4,5},{5,6},{6,7},{7,0},{8,9},{9,10},{10,1... | collective-permute-start | bytes 1179656 | tf_op jit(solution)/shard_map/ppermute | solution.py:210
  114.4 15.3 %collective-permute-start.5 = (bf16[256,768]{1,0:T(8,128)(2,1)S(1)}, bf16[256,768]{1,0:T(8,128)(2,1)S(1)}, u32[]{:S(2)}, u32[]{:S(2)}) collective-permute-start(bf16[256,768]{1,0:T(8,128)(2,1)S(1)} %add_convert_fusion.6), channel_id=1, source_target_pairs={{0,7},{1,0},{2,1},{3,2},{4,3},{5,4},{6,5},{7,6},{8,15},{9,8},{10,9... | collective-permute-start | bytes 1179656 | tf_op jit(solution)/shard_map/ppermute | solution.py:212
  115.8 22.4 %collective-permute-start.8 = (bf16[256,768]{1,0:T(8,128)(2,1)S(1)}, bf16[256,768]{1,0:T(8,128)(2,1)S(1)}, u32[]{:S(2)}, u32[]{:S(2)}) collective-permute-start(bf16[256,768]{1,0:T(8,128)(2,1)S(1)} %add_convert_fusion.4), channel_id=1, source_target_pairs={{0,7},{1,0},{2,1},{3,2},{4,3},{5,4},{6,5},{7,6},{8,15},{9,8},{10,9... | collective-permute-start | bytes 1179656 | tf_op jit(solution)/shard_map/ppermute | solution.py:210
  117.7 21.7 %collective-permute-start.12 = (bf16[256,768]{1,0:T(8,128)(2,1)S(1)}, bf16[256,768]{1,0:T(8,128)(2,1)S(1)}, u32[]{:S(2)}, u32[]{:S(2)}) collective-permute-start(bf16[256,768]{1,0:T(8,128)(2,1)S(1)} %add_convert_fusion.1), channel_id=1, source_target_pairs={{0,1},{1,2},{2,3},{3,4},{4,5},{5,6},{6,7},{7,0},{8,9},{9,10},{10,1... | collective-permute-start | bytes 1179656 | tf_op jit(solution)/shard_map/ppermute | solution.py:212
  121.3 37.9 %collective-permute-start.16 = (bf16[256,512]{1,0:T(8,128)(2,1)S(1)}, bf16[256,512]{1,0:T(8,128)(2,1)S(1)}, u32[]{:S(2)}, u32[]{:S(2)}) collective-permute-start(bf16[256,512]{1,0:T(8,128)(2,1)S(1)} %add_convert_fusion.13), channel_id=1, source_target_pairs={{0,1},{1,2},{2,3},{3,4},{4,5},{5,6},{6,7},{7,0},{8,9},{9,10},{10,1... | collective-permute-start | bytes 786440 | tf_op jit(solution)/shard_map/ppermute | solution.py:210
  126.1 36.5 %collective-permute-start.20 = (bf16[256,512]{1,0:T(8,128)(2,1)S(1)}, bf16[256,512]{1,0:T(8,128)(2,1)S(1)}, u32[]{:S(2)}, u32[]{:S(2)}) collective-permute-start(bf16[256,512]{1,0:T(8,128)(2,1)S(1)} %add_convert_fusion.10), channel_id=1, source_target_pairs={{0,7},{1,0},{2,1},{3,2},{4,3},{5,4},{6,5},{7,6},{8,15},{9,8},{10,9... | collective-permute-start | bytes 786440 | tf_op jit(solution)/shard_map/ppermute | solution.py:212
  129.8 18.6 %collective-permute-start.2 = (bf16[256,768]{1,0:T(8,128)(2,1)S(1)}, bf16[256,768]{1,0:T(8,128)(2,1)S(1)}, u32[]{:S(2)}, u32[]{:S(2)}) collective-permute-start(bf16[256,768]{1,0:T(8,128)(2,1)S(1)} %add_convert_fusion.8), channel_id=1, source_target_pairs={{0,1},{1,2},{2,3},{3,4},{4,5},{5,6},{6,7},{7,0},{8,9},{9,10},{10,1... | collective-permute-start | bytes 1179656 | tf_op jit(solution)/shard_map/ppermute | solution.py:210
  138.2 37.5 %collective-permute-start.6 = (bf16[256,768]{1,0:T(8,128)(2,1)S(1)}, bf16[256,768]{1,0:T(8,128)(2,1)S(1)}, u32[]{:S(2)}, u32[]{:S(2)}) collective-permute-start(bf16[256,768]{1,0:T(8,128)(2,1)S(1)} %add_convert_fusion.5), channel_id=1, source_target_pairs={{0,7},{1,0},{2,1},{3,2},{4,3},{5,4},{6,5},{7,6},{8,15},{9,8},{10,9... | collective-permute-start | bytes 1179656 | tf_op jit(solution)/shard_map/ppermute | solution.py:212
  139.5 19.7 %collective-permute-start.9 = (bf16[256,768]{1,0:T(8,128)(2,1)S(1)}, bf16[256,768]{1,0:T(8,128)(2,1)S(1)}, u32[]{:S(2)}, u32[]{:S(2)}) collective-permute-start(bf16[256,768]{1,0:T(8,128)(2,1)S(1)} %add_convert_fusion.3), channel_id=1, source_target_pairs={{0,7},{1,0},{2,1},{3,2},{4,3},{5,4},{6,5},{7,6},{8,15},{9,8},{10,9... | collective-permute-start | bytes 1179656 | tf_op jit(solution)/shard_map/ppermute | solution.py:210
  139.6 36.1 %copy-start.3 = (bf16[1,256,2048]{2,1,0:T(8,128)(2,1)S(1)}, bf16[1,256,2048]{2,1,0:T(8,128)(2,1)}, u32[]{:S(2)}) copy-start(bf16[1,256,2048]{2,1,0:T(8,128)(2,1)} %param.13) | copy-start | bytes 3145732
  148.3 27.3 %collective-permute-start.13 = (bf16[256,768]{1,0:T(8,128)(2,1)S(1)}, bf16[256,768]{1,0:T(8,128)(2,1)S(1)}, u32[]{:S(2)}, u32[]{:S(2)}) collective-permute-start(bf16[256,768]{1,0:T(8,128)(2,1)S(1)} %add_convert_fusion), channel_id=1, source_target_pairs={{0,1},{1,2},{2,3},{3,4},{4,5},{5,6},{6,7},{7,0},{8,9},{9,10},{10,1... | collective-permute-start | bytes 1179656 | tf_op jit(solution)/shard_map/ppermute | solution.py:212
  159.2 16.5 %collective-permute-start.3 = (bf16[256,768]{1,0:T(8,128)(2,1)S(1)}, bf16[256,768]{1,0:T(8,128)(2,1)S(1)}, u32[]{:S(2)}, u32[]{:S(2)}) collective-permute-start(bf16[256,768]{1,0:T(8,128)(2,1)S(1)} %add_convert_fusion.7), channel_id=1, source_target_pairs={{0,1},{1,2},{2,3},{3,4},{4,5},{5,6},{6,7},{7,0},{8,9},{9,10},{10,1... | collective-permute-start | bytes 1179656 | tf_op jit(solution)/shard_map/ppermute | solution.py:210
  159.3 16.4 %collective-permute-start.10 = (bf16[256,768]{1,0:T(8,128)(2,1)S(1)}, bf16[256,768]{1,0:T(8,128)(2,1)S(1)}, u32[]{:S(2)}, u32[]{:S(2)}) collective-permute-start(bf16[256,768]{1,0:T(8,128)(2,1)S(1)} %add_convert_fusion.2), channel_id=1, source_target_pairs={{0,7},{1,0},{2,1},{3,2},{4,3},{5,4},{6,5},{7,6},{8,15},{9,8},{10,9... | collective-permute-start | bytes 1179656 | tf_op jit(solution)/shard_map/ppermute | solution.py:210
  162.7 13.0 %collective-permute-start.17 = (bf16[256,512]{1,0:T(8,128)(2,1)S(1)}, bf16[256,512]{1,0:T(8,128)(2,1)S(1)}, u32[]{:S(2)}, u32[]{:S(2)}) collective-permute-start(bf16[256,512]{1,0:T(8,128)(2,1)S(1)} %add_convert_fusion.12), channel_id=1, source_target_pairs={{0,1},{1,2},{2,3},{3,4},{4,5},{5,6},{6,7},{7,0},{8,9},{9,10},{10,1... | collective-permute-start | bytes 786440 | tf_op jit(solution)/shard_map/ppermute | solution.py:210
